TPU v7x, 1024 devices: a whole 4x4x32 slice. The times are simulated.
1024 devices in a mesh: clip: 16 (over y, z_hi), seq: 64 (over x, z_lo, core).
Axes of the slice: x: 4, y: 4, z: 32 (z_hi: 4, z_lo: 8; z = z_hi * 8 + z_lo), core: 2. Of those that a mesh axis runs over, the one named last changes fastest.
Arguments:
- hidden_activation: bfloat16 [16, 8192, 1024], P('clip', 'seq'), may hold values from -6 to 6
- projection_weight: bfloat16 [1024, 1536], replicated, may hold values from -0.1875 to 0.1875
- projection_bias: float32 [1536], replicated, may hold values from -6 to 6
- patch_feats: bfloat16 [16, 16384, 1536], P('clip', 'seq'), may hold values from -6 to 6
- pool_slot: int32 [16, 16384], P('clip', 'seq'), may hold values from 0 to 1, as said below
- token_order: int32 [16, 8192], P('clip', 'seq'), may hold values from 0 to 127, as said below
- cos_cotangent: float32 [16, 8192], P('clip', 'seq'), may hold values from -24 to 24
Outputs:
- cos_sim: float32 [16, 8192], P('clip', 'seq')
- weight_grad: float32 [1024, 1536], P('clip')
- bias_grad: float32 [1536], P('clip')
Inputs may be any that keep to these rules, and one draw needn't show every extreme that they name: `pool_slot`: patches come in aligned blocks of 4; each block names every slot 0 to 1 at least once. `token_order`: each aligned block of 128 entries is a permutation of 0 to 127.
All inputs are finite; a program needn't handle non-finite values.
Results may differ from a plain program's by a relative error of at most 0.025.
Values may be sent and summed in bfloat16 or wider, within the bound.
No kernel may reach another device: no remote copies, remote signals or barrier semaphores. Data moves between devices by JAX's collectives and lax.ppermute only.
A program may use at most 64 MiB of HBM per device.

v0:
```python
import jax
import jax.numpy as jnp
from jax import lax
from jax.sharding import PartitionSpec as P


def pool_blocks(patches, slot_ids, slot_count):
    levels = jnp.arange(slot_count, dtype=jnp.int32)
    matches = slot_ids[:, None, :] == levels[None, :, None]
    onehot = matches.astype(jnp.bfloat16)
    totals = jnp.einsum("jlp,jpd->jld", onehot, patches, preferred_element_type=jnp.float32)
    counts = jnp.sum(matches.astype(jnp.float32), axis=2)
    return (totals / counts[:, :, None]).astype(jnp.bfloat16)


def rounded(values):
    return lax.optimization_barrier(values.astype(jnp.bfloat16)).astype(jnp.float32)


def local(
    hidden_activation,
    projection_weight,
    projection_bias,
    patch_feats,
    pool_slot,
    token_order,
    cos_cotangent,
):
    seq_count = lax.axis_size("seq")
    transformer_rows = hidden_activation[0]
    latent_count = transformer_rows.shape[0]
    feature_width = projection_weight.shape[1]
    slot_count = latent_count // seq_count
    patch_count = patch_feats.shape[1]
    per_block = patch_count // seq_count
    projected_rows = (
        jnp.dot(transformer_rows, projection_weight, preferred_element_type=jnp.float32)
        + projection_bias
    )
    moved_feats, moved_slots = (
        lax.all_to_all(patch_feats[0], "seq", split_axis=0, concat_axis=0, tiled=True),
        lax.all_to_all(pool_slot[0], "seq", split_axis=0, concat_axis=0, tiled=True),
    )
    arrived = pool_blocks(
        moved_feats.reshape(seq_count, per_block, feature_width),
        moved_slots.reshape(seq_count, per_block),
        slot_count,
    )
    arrived = arrived.reshape(latent_count, feature_width)
    target = jnp.take(arrived, token_order[0], axis=0).astype(jnp.float32)
    inv_proj = lax.rsqrt(jnp.sum(projected_rows * projected_rows, axis=1) + 1e-06)
    inv_target = lax.rsqrt(jnp.sum(target * target, axis=1) + 1e-06)
    cosine = jnp.sum(projected_rows * target, axis=1) * inv_proj * inv_target
    gradient_rows_local = cos_cotangent[0][:, None] * (
        target * (inv_proj * inv_target)[:, None]
        - (cosine * inv_proj * inv_proj)[:, None] * projected_rows
    )
    gradient_rows_local = gradient_rows_local.astype(jnp.bfloat16)
    weight_portion = lax.dot_general(
        transformer_rows,
        gradient_rows_local,
        (((0,), (0,)), ((), ())),
        preferred_element_type=jnp.float32,
    )
    weight_round = rounded(weight_portion)
    bias_round = rounded(jnp.sum(gradient_rows_local.astype(jnp.float32), axis=0))
    weight_share, bias_share = (
        lax.psum_scatter(
            weight_round.astype(jnp.bfloat16), "clip", scatter_dimension=0, tiled=True
        ).astype(jnp.float32),
        lax.psum_scatter(
            bias_round.astype(jnp.bfloat16), "clip", scatter_dimension=0, tiled=True
        ).astype(jnp.float32),
    )
    weight_grad, bias_grad = lax.psum((weight_share, bias_share), "seq")
    return (cosine[None, :], weight_grad, bias_grad)


def solution(mesh):
    placed = (
        P("clip", "seq", None),
        P(),
        P(),
        P("clip", "seq", None),
        P("clip", "seq"),
        P("clip", "seq"),
        P("clip", "seq"),
    )
    return jax.shard_map(
        local,
        mesh=mesh,
        in_specs=placed,
        out_specs=(P("clip", "seq"), P("clip", None), P("clip")),
        check_vma=False,
    )
```

profile of v0, /device:TPU:1, one launch (start us, length us, event | category | flops | bytes accessed | tf_op | source)
XLA Modules:
  0.0 783.6 jit_solution(9202734084774187986)
XLA Ops:
  7.2 0.0 copy-start
  7.2 0.0 copy-start.5
  7.2 0.5 broadcast.80
  7.7 1.4 reduce.4
  9.1 0.7 all_to_all.12
  9.8 18.2 %all-to-all-start = ((s32[64,4,1]{1,2,0:T(1,128)}), s32[64,4,1]{1,2,0:T(1,128)S(1)}, u32[]{:S(2)}, u32[]{:S(2)}) async-start(s32[64,4,1]{1,2,0:T(1,128)} %bitcast.2), calls=%async_computation | async-start | bytes 65536 | tf_op jit(solution)/shard_map/all_to_all | solution.py:42
  28.0 2.4 all_to_all.14
  30.4 9.9 %all-to-all-done = s32[64,4,1]{1,2,0:T(1,128)S(1)} async-done(((s32[64,4,1]{1,2,0:T(1,128)}), s32[64,4,1]{1,2,0:T(1,128)S(1)}, u32[]{:S(2)}, u32[]{:S(2)}) %all-to-all-start) | async-done | bytes 1056 | tf_op jit(solution)/shard_map/all_to_all | solution.py:42
  40.3 5.5 all-to-all-start.1
  45.8 0.0 reduce-scatter.4.cloned.1.call-start
  45.8 0.0 copy-done.5
  45.9 0.1 convert_reduce_fusion
  46.0 39.8 %all-to-all-done.1 = bf16[64,4,1536]{2,1,0:T(4,128)(2,1)} async-done(((bf16[64,4,1536]{2,1,0:T(4,128)(2,1)}), bf16[64,4,1536]{2,1,0:T(4,128)(2,1)}, u32[]{:S(2)}, u32[]{:S(2)}) %all-to-all-start.1) | async-done | bytes 786464 | tf_op jit(solution)/shard_map/all_to_all | solution.py:41
  85.8 2.4 fusion.1
  88.3 0.0 copy-start.4
  88.3 1.2 reshape.113
  89.4 1.6 gather_fusion
  91.1 0.0 copy-done
  91.1 0.0 copy-done.4
  91.1 0.0 copy-start.1
  91.1 0.0 copy-start.3
  91.1 0.0 copy-start.2
  91.1 1.9 multiply_reduce_fusion
  93.0 0.5 multiply_multiply_fusion
  93.5 0.0 copy-done.1
  93.5 0.0 copy-done.3
  93.5 0.3 fusion.12
  93.8 0.0 copy-done.2
  93.8 2.7 fusion
  96.5 4.6 copy.14
  101.2 0.0 reduce-scatter.4.cloned.1.call-update
  101.2 1.3 dynamic-slice
  103.1 82.0 %all-reduce = bf16[1536]{0:T(1024)(128)(2,1)S(1)} all-reduce(bf16[1536]{0:T(1024)(128)(2,1)S(1)} %get-tuple-element.17), channel_id=3, replica_groups=mesh['clip'=16,'seq'=64] {'clip'}, use_global_device_ids=true, to_apply=%region_7.8.clone | all-reduce | flops 1536 | bytes 6144
  185.1 0.1 dynamic-slice_convert_fusion
  185.2 162.6 %reduce-scatter.4.cloned.1.call-done = bf16[64,1536]{1,0:T(8,128)(2,1)} async-done(((bf16[1024,1536]{1,0:T(8,128)(2,1)}), bf16[64,1536]{1,0:T(8,128)(2,1)}) %reduce-scatter.4.cloned.1.call-update) | async-done | bytes 196624
  347.8 1.1 copy.15
  349.0 425.7 %all-reduce.3 = (f32[64,1536]{0,1:T(8,128)}, f32[96]{0:T(128)}) all-reduce(bf16[64,1536]{0,1:T(8,128)(2,1)S(1)} %copy.15, f32[96]{0:T(128)S(1)} %dynamic-slice_convert_fusion), channel_id=1, replica_groups=mesh['clip'=16,'seq'=64] {'seq'}, use_global_device_ids=true, to_apply=%region_5.6 | all-reduce | flops 98400 | bytes 590592 | tf_op jit(solution)/shard_map/psum | solution.py:75
  774.7 2.1 copy.13
  (3 shorter events, 0.0 us)
Async XLA Ops:
  7.2 83.9 %copy-start = (bf16[1024,1536]{1,0:T(8,128)(2,1)S(1)}, bf16[1024,1536]{1,0:T(8,128)(2,1)}, u32[]{:S(2)}) copy-start(bf16[1024,1536]{1,0:T(8,128)(2,1)} %param.8) | copy-start | bytes 9437188
  7.2 38.6 %copy-start.5 = (s32[1,128]{1,0:T(1,128)S(1)}, s32[1,128]{1,0:T(1,128)}, u32[]{:S(2)}) copy-start(s32[1,128]{1,0:T(1,128)} %param.12) | copy-start | bytes 1540
  9.8 30.5 %all-to-all-start = ((s32[64,4,1]{1,2,0:T(1,128)}), s32[64,4,1]{1,2,0:T(1,128)S(1)}, u32[]{:S(2)}, u32[]{:S(2)}) async-start(s32[64,4,1]{1,2,0:T(1,128)} %bitcast.2), calls=%async_computation | async-start | bytes 65536 | tf_op jit(solution)/shard_map/all_to_all | solution.py:42
  40.3 45.6 %all-to-all-start.1 = ((bf16[64,4,1536]{2,1,0:T(4,128)(2,1)}), bf16[64,4,1536]{2,1,0:T(4,128)(2,1)}, u32[]{:S(2)}, u32[]{:S(2)}) async-start(bf16[64,4,1536]{2,1,0:T(4,128)(2,1)} %all_to_all.14), calls=%async_computation.1 | async-start | bytes 1572864 | tf_op jit(solution)/shard_map/all_to_all | solution.py:41
  45.8 302.1 %reduce-scatter.4.cloned.1.call-start = ((), (), s32[]{:S(2)}) async-start(), calls=%async_computation.3 | async-start | bytes 3342336
  88.3 2.8 copy-start.4
  91.1 2.4 copy-start.1
  91.1 2.4 copy-start.3
  91.1 2.7 copy-start.2
Sparse Core Ops, SparseCore 0:
  101.3 246.4 reduce-scatter.3
where the time goes:
time: 794 us; the launch traced here: 784 us
  blocking collectives  508 us (64%)
  waiting for transfers between devices  212 us (27%)
  starting transfers between devices  23.7 us (3%)
  local copies, waits for them, and re-layouts  15.7 us (2%)
  between operations  14.8 us (2%)
    psum x1, blocking collectives, local(): weight_grad, bias_grad = lax.psum((weight_share, bias_share), 'seq')  426 us
    unnamed x2, waiting for transfers between devices  163 us
    unnamed x1, blocking collectives  82 us
    all_to_all x1, waiting for transfers between devices, local(): lax.all_to_all(patch_feats[0], 'seq', split_axis=0, concat_axis=0, tiled=...  39.8 us
    all_to_all x1, starting transfers between devices, local(): lax.all_to_all(pool_slot[0], 'seq', split_axis=0, concat_axis=0, tiled=True)  18.2 us
  transfers between devices with their start and end apart: 3, of which 3 were waited for; matrix products, arithmetic and copies ran while one was open for 0% of the time, Pallas kernels for 0%

commit v1 on v0

v1 whole, which is shorter than its diff:
```python
import jax
import jax.numpy as jnp
from jax import lax
from jax.sharding import Mesh, PartitionSpec as P

BF = jnp.bfloat16
F32 = jnp.float32
LANES = 128


def split_terms(values, terms):
    parts = []
    for _ in range(terms - 1):
        head = lax.reduce_precision(values, 8, 7)
        parts.append(head.astype(BF))
        values = values - head
    parts.append(values.astype(BF))
    return parts


def join_terms(parts):
    total = parts[-1].astype(F32)
    for part in parts[-2::-1]:
        total = total + part.astype(F32)
    return total


def local(hidden, weight, bias, patches, slots, order, cotangent):
    y_n, h_n, x_n, l_n, c_n = (lax.axis_size(a) for a in ("y", "h", "x", "l", "c"))
    hidden, patches = hidden[0], patches[0]
    slots, order, cotangent = slots[0], order[0], cotangent[0]
    tokens, units = hidden.shape
    width = weight.shape[1]
    patch_count = patches.shape[0]
    near = x_n * l_n
    per = tokens // near
    shards = near * c_n
    two = tokens // shards
    block = patch_count // shards
    half = width // c_n
    rows = units // (y_n * h_n)
    own = rows // near
    core = lax.axis_index("c")

    pick = order[None, :] == jnp.arange(tokens, dtype=jnp.int32)[:, None]
    sent_rows = jnp.dot(pick.astype(BF), hidden, preferred_element_type=F32).astype(BF)
    sent_cot = jnp.sum(jnp.where(pick, cotangent[None, :], 0.0), axis=1)
    cot_cols = jnp.stack(split_terms(sent_cot, 3), axis=1)
    cot_cols = jnp.pad(cot_cols, ((0, 0), (0, LANES - 3)))
    sent = jnp.concatenate([sent_rows, cot_cols], axis=1).reshape(near, per, units + LANES)
    moved = lax.all_to_all(sent, ("x", "l"), 0, 0, tiled=True)

    at = jnp.arange(tokens, dtype=jnp.int32)
    src_core, src_chip, level = at // (near * two), (at // two) % near, at % two
    src = src_chip * c_n + src_core
    q = jnp.arange(patch_count, dtype=jnp.int32)
    match = (q[None, :] // block == src[:, None]) & (slots[None, :] == level[:, None])
    totals = jnp.dot(match.astype(BF), patches, preferred_element_type=F32)
    counts = jnp.sum(match.astype(F32), axis=1)
    pooled = (totals / counts[:, None]).astype(BF)
    target = lax.all_gather(pooled, "c", axis=0, tiled=True)
    target = target.reshape(c_n, shards, two, width).transpose(1, 0, 2, 3)
    target = target.reshape(c_n * tokens, width).astype(F32)

    both = lax.all_gather(moved, "c", axis=0, tiled=True).reshape(c_n * tokens, units + LANES)
    acts = both[:, :units]
    cot = join_terms([both[:, units + k] for k in range(3)])
    projected = jnp.dot(acts, weight, preferred_element_type=F32) + bias
    inv_proj = lax.rsqrt(jnp.sum(projected * projected, axis=1) + 1e-06)
    inv_target = lax.rsqrt(jnp.sum(target * target, axis=1) + 1e-06)
    cosine = jnp.sum(projected * target, axis=1) * inv_proj * inv_target
    grads = cot[:, None] * (
        target * (inv_proj * inv_target)[:, None] - (cosine * inv_proj * inv_proj)[:, None] * projected
    )
    grads = grads.astype(BF)
    grads_half = lax.dynamic_slice_in_dim(grads, core * half, half, axis=1)
    part = lax.dot_general(acts, grads_half, (((0,), (0,)), ((), ())), preferred_element_type=F32)
    part = part.astype(BF).reshape(y_n, h_n, x_n, rows // x_n, half).transpose(0, 2, 1, 3, 4)
    part = part.reshape(y_n * x_n, h_n * rows // x_n, half)
    cols = width // (y_n * h_n)
    bias_part = jnp.sum(grads.astype(F32), axis=0).astype(BF).reshape(y_n * x_n, 1, cols)
    bias_part = jnp.pad(bias_part, ((0, 0), (0, 7), (0, half - cols)))
    part = jnp.concatenate([part, bias_part], axis=1)

    part = lax.all_to_all(part, ("y", "x"), 0, 0, tiled=True)
    plane = jnp.sum(part.astype(F32), axis=0)
    lines = own * half // LANES
    plane_w = plane[:-8].astype(BF).reshape(h_n * l_n, lines, LANES)
    plane_b = jnp.pad(jnp.stack(split_terms(plane[-8, :cols], 2)), ((0, 14 - lines), (0, LANES - cols)))
    plane_b = jnp.broadcast_to(plane_b, (h_n * l_n, 16 - lines, LANES))
    part = jnp.concatenate([plane_w, plane_b], axis=1)
    part = lax.all_to_all(part, ("h", "l"), 0, 0, tiled=True).astype(F32)
    full_w = jnp.sum(part[:, :lines], axis=0).astype(BF)
    full_b = jnp.sum(part[:, lines] + part[:, lines + 1], axis=0)

    back = lax.dynamic_slice_in_dim(cosine.reshape(c_n, near, per), core, 1, axis=0)[0]
    back = jnp.pad(jnp.stack(split_terms(back, 2), axis=1), ((0, 0), (0, 0), (0, LANES - per)))
    ahead = jnp.concatenate([full_w, jnp.stack(split_terms(full_b, 2))], axis=0)
    ahead = jnp.broadcast_to(ahead, (near, lines + 2, LANES))
    part = lax.all_to_all(jnp.concatenate([ahead, back], axis=1), ("x", "l"), 0, 0, tiled=True)
    block_w = part[:, :lines].reshape(rows, half)
    weight_grad = lax.all_gather(block_w, "c", axis=1, tiled=True).astype(F32)
    mine = lax.dynamic_slice_in_dim(part, lax.axis_index("h") * l_n, 1, axis=0)[0]
    bias_grad = (mine[lines].astype(F32) + mine[lines + 1].astype(F32))[:cols]
    by_slot = (part[:, lines + 2].astype(F32) + part[:, lines + 3].astype(F32))[:, :per].reshape(tokens)
    cos_out = jnp.sum(jnp.where(pick, by_slot[:, None], 0.0), axis=0)
    return cos_out[None, :], weight_grad, bias_grad


def solution(mesh, sizes=(4, 4, 4, 8, 2)):
    fine = Mesh(mesh.devices.reshape(sizes), ("y", "h", "x", "l", "c"))
    clip, seq = ("y", "h"), ("x", "l", "c")
    placed = (
        P(clip, seq, None),
        P(),
        P(),
        P(clip, seq, None),
        P(clip, seq),
        P(clip, seq),
        P(clip, seq),
    )
    return jax.shard_map(
        local,
        mesh=fine,
        in_specs=placed,
        out_specs=(P(clip, seq), P(clip, None), P(clip)),
        check_vma=False,
    )
```

time: 794 us -> 159 us (0.20); the launches traced: 784 us -> 158 us
  blocking collectives: 508 us -> 43 us
  waiting for transfers between devices: 212 us -> 41.8 us
  starting transfers between devices: 23.7 us -> 41 us
  between operations: 14.8 us -> 0.94 us
    psum x1 -> x0, blocking collectives: 426 us -> none  [local(): weight_grad, bias_grad = lax.psum((weight_share, bias_share), 'seq')]
    unnamed x2 -> x0, waiting for transfers between devices: 163 us -> none
    unnamed x1 -> x0, blocking collectives: 82 us -> none
    all_to_all x0 -> x1, blocking collectives: none -> 28.7 us  [local(): part = lax.all_to_all(part, ('y', 'x'), 0, 0, tiled=True)]
    all_to_all x2 -> x3, starting transfers between devices: 23.7 us -> 41 us  [the longest x1 21 us: local(): part = lax.all_to_all(part, ('h', 'l'), 0, 0, tiled=True).astype(F32)]
    all_gather x0 -> x3, blocking collectives: none -> 14.3 us  [the longest x1 6.24 us: local(): weight_grad = lax.all_gather(block_w, 'c', axis=1, tiled=True).astype(F32)]
    unnamed x17 -> x12, local copies, waits for them, and re-layouts: 9.74 us -> 0.23 us
    convert_element_type x0 -> x3, local copies, waits for them, and re-layouts: none -> 8.8 us  [local(): target = target.reshape(c_n * tokens, width).astype(F32)]
  transfers between devices with their start and end apart: 3 -> 3, of which waited for: 3 -> 3; matrix products, arithmetic and copies ran while one was open for 0% -> 9% of each run, Pallas kernels for 0% -> 0%
where the time goes in v1:
time: 159 us; the launch traced here: 158 us
  blocking collectives  43 us (27%)
  waiting for transfers between devices  41.8 us (26%)
  starting transfers between devices  41 us (26%)
  local copies, waits for them, and re-layouts  15.4 us (10%)
  other arithmetic  8.37 us (5%)
  matrix products  7.25 us (5%)
    all_to_all x1, blocking collectives, local(): part = lax.all_to_all(part, ('y', 'x'), 0, 0, tiled=True)  28.7 us
    all_to_all x1, waiting for transfers between devices, local(): part = lax.all_to_all(part, ('h', 'l'), 0, 0, tiled=True).astype(F32)  28 us
    all_to_all x1, starting transfers between devices, local(): part = lax.all_to_all(part, ('h', 'l'), 0, 0, tiled=True).astype(F32)  21 us
    all_to_all x1, starting transfers between devices, local(): moved = lax.all_to_all(sent, ('x', 'l'), 0, 0, tiled=True)  15.9 us
    all_to_all x1, waiting for transfers between devices, local(): lax.all_to_all(jnp.concatenate([ahead, back], axis=1), ('x', 'l'), 0, 0,...  11.8 us
    convert_element_type x3, local copies, waits for them, and re-layouts, local(): target = target.reshape(c_n * tokens, width).astype(F32)  8.8 us
    all_gather x1, blocking collectives, local(): weight_grad = lax.all_gather(block_w, 'c', axis=1, tiled=True).astype(F32)  6.24 us
    all_gather x1, blocking collectives, local(): target = lax.all_gather(pooled, 'c', axis=0, tiled=True)  4.23 us
  transfers between devices with their start and end apart: 3, of which 3 were waited for; matrix products, arithmetic and copies ran while one was open for 9% of the time, Pallas kernels for 0%

profile of v1, /device:TPU:1, one launch (start us, length us, event | category | flops | bytes accessed | tf_op | source)
XLA Modules:
  0.0 157.8 jit_solution(6958936312539350676)
XLA Ops:
  0.6 0.0 copy-start
  0.7 0.9 select_reduce_fusion.1
  1.6 0.1 copy.44
  1.8 1.2 convolution_convert_fusion.1
  3.0 0.8 reshape.253
  3.8 15.9 %all-to-all-start = ((bf16[32,4,1152]{2,1,0:T(4,128)(2,1)}), bf16[32,4,1152]{2,1,0:T(4,128)(2,1)S(1)}, u32[]{:S(2)}, u32[]{:S(2)}) async-start(bf16[32,4,1152]{2,1,0:T(4,128)(2,1)} %reshape.253), calls=%async_computation | async-start | bytes 589824 | tf_op jit(solution)/shard_map/all_to_all | solution.py:51
  19.7 0.2 convert_reduce_fusion.1
  19.9 1.5 fusion.1
  21.4 4.2 %all_gather.10 = bf16[256,1536]{1,0:T(8,128)(2,1)} all-gather(bf16[128,1536]{1,0:T(8,128)(2,1)S(1)} %fusion.1), channel_id=1, replica_groups=mesh['y'=4,'h'=4,'x'=4,'l'=8,'c'=2] {'c'}, dimensions={0}, use_global_device_ids=true | all-gather | bytes 1179648 | tf_op jit(solution)/shard_map/all_gather | solution.py:61
  25.6 3.0 %reshape.264 = f32[2,64,2,1536]{3,2,1,0:T(2,128)} reshape(bf16[256,1536]{1,0:T(8,128)(2,1)} %all_gather.10) | data formatting | bytes 2359296 | tf_op jit(solution)/shard_map/convert_element_type | solution.py:63
  28.6 1.4 multiply_reduce_fusion.1
  30.0 0.1 reshape.263
  30.1 0.7 copy.46
  30.8 1.0 rsqrt.31
  31.8 2.7 %copy.45 = f32[64,2,2,1536]{3,2,1,0:T(2,128)} copy(f32[64,2,2,1536]{3,2,0,1:T(2,128)} %bitcast.37) | data formatting | bytes 3145728 | tf_op jit(solution)/shard_map/convert_element_type | solution.py:63
  34.4 3.2 %reshape.260 = f32[256,1536]{1,0:T(8,128)} reshape(f32[64,2,2,1536]{3,2,1,0:T(2,128)} %copy.45) | data formatting | bytes 3145728 | tf_op jit(solution)/shard_map/convert_element_type | solution.py:63
  37.6 2.1 %all-to-all-done = bf16[32,4,1152]{2,1,0:T(4,128)(2,1)S(1)} async-done(((bf16[32,4,1152]{2,1,0:T(4,128)(2,1)}), bf16[32,4,1152]{2,1,0:T(4,128)(2,1)S(1)}, u32[]{:S(2)}, u32[]{:S(2)}) %all-to-all-start) | async-done | bytes 294944 | tf_op jit(solution)/shard_map/all_to_all | solution.py:51
  39.7 3.8 %all_gather.9 = bf16[64,4,1152]{2,1,0:T(4,128)(2,1)} all-gather(bf16[32,4,1152]{2,1,0:T(4,128)(2,1)S(1)} %all-to-all-done), channel_id=1, replica_groups=mesh['y'=4,'h'=4,'x'=4,'l'=8,'c'=2] {'c'}, dimensions={0}, use_global_device_ids=true | all-gather | bytes 884736 | tf_op jit(solution)/shard_map/all_gather | solution.py:65
  43.5 2.2 %reshape.254 = bf16[256,1152]{1,0:T(8,128)(2,1)} reshape(bf16[64,4,1152]{2,1,0:T(4,128)(2,1)} %all_gather.9) | data formatting | bytes 1179648 | tf_op jit(solution)/shard_map/reshape | solution.py:65
  45.7 1.2 add_reduce_fusion
  46.9 2.8 %multiply_reduce_fusion.2 = (f32[256]{0:T(256)S(1)}, f32[256]{0:T(256)S(1)}, f32[256,1536]{1,0:T(8,128)S(1)}) fusion(f32[256,1536]{1,0:T(8,128)} %reshape.260, f32[1536]{0:T(1024)S(1)} %copy-done.2, bf16[1024,1536]{1,0:T(8,128)(2,1)S(1)} %copy-done, bf16[256,1152]{1,0:T(8,128)(2,1)} %reshape.254), kind=kOutput, calls=%fused_computation.11 | convolution fusion | flops 807271936 | bytes 6823936 | tf_op jit(solution)/shard_map/dot_general | solution.py:68
  49.8 1.3 fusion.38
  51.0 0.1 reshape.265
  51.1 1.8 %convolution_convert_fusion = bf16[1024,768]{1,0:T(8,128)(2,1)S(1)} fusion(bf16[256,1152]{1,0:T(8,128)(2,1)} %reshape.254, bf16[256,1536]{1,0:T(8,128)(2,1)} %get-tuple-element.6, s32[]{:T(128)S(6)} %select_n.68), kind=kOutput, calls=%fused_computation.7 | convolution fusion | flops 403439616 | bytes 2490372 | tf_op jit(solution)/shard_map/dot_general | solution.py:77
  52.9 0.1 copy.47
  53.1 0.1 fusion.2
  53.2 28.7 %all_to_all.20 = bf16[16,72,768]{2,1,0:T(8,128)(2,1)S(1)} all-to-all(bf16[16,72,768]{2,1,0:T(8,128)(2,1)S(1)} %fusion.2), channel_id=1, replica_groups=mesh['y'=4,'h'=4,'x'=4,'l'=8,'c'=2] {'y','x'}, dimensions={0} | all-to-all | bytes 3538944 | tf_op jit(solution)/shard_map/all_to_all | solution.py:85
  81.9 0.2 convert_reduce_fusion
  82.2 0.1 reshape.258
  82.3 0.7 pad_maximum_fusion
  83.0 21.0 %all-to-all-start.2 = ((bf16[32,16,128]{2,1,0:T(8,128)(2,1)}), bf16[32,16,128]{2,1,0:T(8,128)(2,1)S(1)}, u32[]{:S(2)}, u32[]{:S(2)}) async-start(bf16[32,16,128]{2,1,0:T(8,128)(2,1)} %pad_maximum_fusion), calls=%async_computation.2 | async-start | bytes 262144 | tf_op jit(solution)/shard_map/all_to_all | solution.py:92
  104.0 0.1 copy.49
  104.1 0.1 rsqrt.32
  104.2 0.1 copy.54
  104.3 0.1 mul.111
  104.4 0.1 copy.51
  104.5 0.1 copy.53
  104.6 28.0 %all-to-all-done.2 = bf16[32,16,128]{2,1,0:T(8,128)(2,1)S(1)} async-done(((bf16[32,16,128]{2,1,0:T(8,128)(2,1)}), bf16[32,16,128]{2,1,0:T(8,128)(2,1)S(1)}, u32[]{:S(2)}, u32[]{:S(2)}) %all-to-all-start.2) | async-done | bytes 131104 | tf_op jit(solution)/shard_map/all_to_all | solution.py:92
  132.6 0.1 fusion.18
  132.8 0.7 fusion.11
  133.5 4.1 %all-to-all-start.3 = ((bf16[32,16,128]{2,1,0:T(8,128)(2,1)}), bf16[32,16,128]{2,1,0:T(8,128)(2,1)S(1)}, u32[]{:S(2)}, u32[]{:S(2)}) async-start(bf16[32,16,128]{2,1,0:T(8,128)(2,1)} %fusion.11), calls=%async_computation.3 | async-start | bytes 262144 | tf_op jit(solution)/shard_map/all_to_all | solution.py:100
  137.6 11.8 %all-to-all-done.3 = bf16[32,16,128]{2,1,0:T(8,128)(2,1)S(1)} async-done(((bf16[32,16,128]{2,1,0:T(8,128)(2,1)}), bf16[32,16,128]{2,1,0:T(8,128)(2,1)S(1)}, u32[]{:S(2)}, u32[]{:S(2)}) %all-to-all-start.3) | async-done | bytes 131104 | tf_op jit(solution)/shard_map/all_to_all | solution.py:100
  149.4 0.1 broadcast_in_dim.49
  149.5 0.6 select_reduce_fusion
  150.2 0.1 reshape.259
  150.3 6.2 %all_gather.11 = bf16[64,1536]{1,0:T(8,128)(2,1)S(1)} all-gather(bf16[64,768]{1,0:T(8,128)(2,1)S(1)} %reshape.259), channel_id=1, replica_groups=mesh['y'=4,'h'=4,'x'=4,'l'=8,'c'=2] {'c'}, dimensions={1}, use_global_device_ids=true | all-gather | bytes 294912 | tf_op jit(solution)/shard_map/all_gather | solution.py:102
  156.5 0.8 convert_element_type.190
  157.3 0.5 slice_bitcast_fusion
  (31 shorter events, 0.3 us)
Async XLA Ops:
  0.6 46.3 %copy-start = (bf16[1024,1536]{1,0:T(8,128)(2,1)S(1)}, bf16[1024,1536]{1,0:T(8,128)(2,1)}, u32[]{:S(2)}) copy-start(bf16[1024,1536]{1,0:T(8,128)(2,1)} %param.8) | copy-start | bytes 9437188
  0.6 19.1 %copy-start.3 = (s32[1,256]{1,0:T(1,128)S(1)}, s32[1,256]{1,0:T(1,128)}, u32[]{:S(2)}) copy-start(s32[1,256]{1,0:T(1,128)} %param.11) | copy-start | bytes 3076
  3.8 35.9 %all-to-all-start = ((bf16[32,4,1152]{2,1,0:T(4,128)(2,1)}), bf16[32,4,1152]{2,1,0:T(4,128)(2,1)S(1)}, u32[]{:S(2)}, u32[]{:S(2)}) async-start(bf16[32,4,1152]{2,1,0:T(4,128)(2,1)} %reshape.253), calls=%async_computation | async-start | bytes 589824 | tf_op jit(solution)/shard_map/all_to_all | solution.py:51
  37.6 9.3 %copy-start.2 = (f32[1536]{0:T(1024)S(1)}, f32[1536]{0:T(1024)}, u32[]{:S(2)}) copy-start(f32[1536]{0:T(1024)} %param.9) | copy-start | bytes 18436
  46.9 2.9 %copy-start.1 = (f32[256,1536]{1,0:T(8,128)S(1)}, f32[256,1536]{1,0:T(8,128)}, u32[]{:S(2)}) copy-start(f32[256,1536]{1,0:T(8,128)} %reshape.260) | copy-start | bytes 4718596
  82.1 67.4 %copy-start.4 = (s32[1,128]{1,0:T(1,128)S(1)}, s32[1,128]{1,0:T(1,128)}, u32[]{:S(2)}) copy-start(s32[1,128]{1,0:T(1,128)} %param.12) | copy-start | bytes 1540
  83.0 49.5 %all-to-all-start.2 = ((bf16[32,16,128]{2,1,0:T(8,128)(2,1)}), bf16[32,16,128]{2,1,0:T(8,128)(2,1)S(1)}, u32[]{:S(2)}, u32[]{:S(2)}) async-start(bf16[32,16,128]{2,1,0:T(8,128)(2,1)} %pad_maximum_fusion), calls=%async_computation.2 | async-start | bytes 262144 | tf_op jit(solution)/shard_map/all_to_all | solution.py:92
  133.5 15.9 %all-to-all-start.3 = ((bf16[32,16,128]{2,1,0:T(8,128)(2,1)}), bf16[32,16,128]{2,1,0:T(8,128)(2,1)S(1)}, u32[]{:S(2)}, u32[]{:S(2)}) async-start(bf16[32,16,128]{2,1,0:T(8,128)(2,1)} %fusion.11), calls=%async_computation.3 | async-start | bytes 262144 | tf_op jit(solution)/shard_map/all_to_all | solution.py:100

commit v2 on v1

v2 whole, which is shorter than its diff:
```python
import functools

import jax
import jax.numpy as jnp
from jax import lax
from jax.experimental import pallas as pl
from jax.experimental.pallas import tpu as pltpu
from jax.sharding import Mesh, PartitionSpec as P

BF = jnp.bfloat16
F32 = jnp.float32
I32 = jnp.int32
LANES = 128
TAIL = 16
LINE_ROWS = 2
VMEM = pl.BlockSpec(memory_space=pltpu.VMEM)
SMEM = pl.BlockSpec(memory_space=pltpu.SMEM)


def iota(shape, axis):
    return lax.broadcasted_iota(I32, shape, axis)


def split_two(values):
    head = values.astype(BF)
    return head, (values - head.astype(F32)).astype(BF)


def call(body, outs, ins, scratch=(), limit=40):
    return pl.pallas_call(
        body,
        out_shape=outs,
        in_specs=ins,
        out_specs=jax.tree.map(lambda _: VMEM, outs),
        scratch_shapes=list(scratch),
        compiler_params=pltpu.CompilerParams(vmem_limit_bytes=limit << 20),
    )


def send_kernel(hidden_ref, order_ref, cot_ref, out_ref):
    tokens, units = hidden_ref.shape
    pick = order_ref[...] == iota((tokens, tokens), 0)
    rows = jnp.dot(
        jnp.where(pick, 1.0, 0.0).astype(BF), hidden_ref[...], preferred_element_type=F32
    )
    out_ref[:, :units] = rows.astype(BF)
    cot = jnp.sum(jnp.where(pick, cot_ref[...], 0.0), axis=1, keepdims=True)
    high = cot.astype(BF).astype(F32)
    rest = cot - high
    middle = rest.astype(BF).astype(F32)
    low = rest - middle
    lane = iota((tokens, LANES), 1)
    cols = jnp.where(lane == 0, high, jnp.where(lane == 1, middle, jnp.where(lane == 2, low, 0.0)))
    out_ref[:, units:] = cols.astype(BF)


def middle_kernel(
    dims, core_ref, both_ref, pooled_ref, weight_ref, bias_ref, part_ref, back_ref, proj, target, grads
):
    y_n, h_n, x_n, l_n, c_n, two = dims
    near, per = x_n * l_n, c_n * two
    tokens, units = both_ref.shape[0], both_ref.shape[1] - LANES
    width = weight_ref.shape[1]
    half = width // c_n
    single = tokens // c_n
    core = core_ref[0]
    row = iota((tokens, tokens), 0)
    wanted = (
        (row // two) % c_n * single + row // single * (near * two) + row // per % near * two + row % two
    )
    turn = jnp.where(wanted == iota((tokens, tokens), 1), 1.0, 0.0).astype(BF)
    acts = both_ref[:, :units]
    step = 256
    s_pp = jnp.zeros((tokens, 1), F32)
    s_tt = jnp.zeros((tokens, 1), F32)
    s_pt = jnp.zeros((tokens, 1), F32)
    for at in range(0, width, step):
        cut = slice(at, at + step)
        p = jnp.dot(acts, weight_ref[:, cut], preferred_element_type=F32) + bias_ref[:, cut]
        t = jnp.dot(turn, pooled_ref[:, cut], preferred_element_type=F32)
        proj[:, cut] = p
        target[:, cut] = t
        s_pp = s_pp + jnp.sum(p * p, axis=1, keepdims=True)
        s_tt = s_tt + jnp.sum(t * t, axis=1, keepdims=True)
        s_pt = s_pt + jnp.sum(p * t, axis=1, keepdims=True)
    inv_proj = lax.rsqrt(s_pp + 1e-06)
    inv_target = lax.rsqrt(s_tt + 1e-06)
    cosine = s_pt * inv_proj * inv_target
    terms = both_ref[:, units:].astype(F32)
    cot = (terms[:, 2:3] + terms[:, 1:2]) + terms[:, 0:1]
    scale_t = inv_proj * inv_target
    scale_p = cosine * inv_proj * inv_proj
    y_blocks = width // y_n // LANES
    tail_row = iota((TAIL, step), 0)
    main = part_ref.shape[1] - TAIL
    for at in range(0, width, step):
        g = cot * (target[:, at : at + step] * scale_t - scale_p * proj[:, at : at + step])
        g = g.astype(BF)
        inside = at % half
        grads[at // half, :, inside : inside + step] = g
        total = jnp.sum(g.astype(F32), axis=0, keepdims=True)
        high = total.astype(BF).astype(F32)
        tail = jnp.where(tail_row == 0, high, jnp.where(tail_row == 1, total - high, 0.0)).astype(BF)
        for k in range(step // LANES):
            block = at // LANES + k
            piece = block // y_blocks * x_n + block % y_blocks
            part_ref[piece, main:, :] = tail[:, k * LANES : (k + 1) * LANES]
    for y in range(y_n):
        for x in range(y_blocks, x_n):
            part_ref[y * x_n + x, main:, :] = jnp.zeros((TAIL, LANES), BF)
    lane = iota((tokens, LANES), 1)
    high, low = split_two(cosine)
    spot = iota((tokens, LANES), 0) % per == lane
    owner = iota((near, tokens), 1) - core * single
    gather = jnp.where((owner >= 0) & (owner < single) & (owner // per == iota((near, tokens), 0)), 1.0, 0.0)
    gather = gather.astype(BF)
    back = jnp.zeros((near, LANES), F32)
    for term in (high, low):
        spread = jnp.where(spot, term.astype(F32), 0.0).astype(BF)
        back = back + jnp.dot(gather, spread, preferred_element_type=F32)
    back_ref[...] = back
    rows = units // y_n
    chunk = rows // h_n // x_n
    mine = grads[core]
    for y in range(y_n):
        product = lax.dot_general(
            acts[:, y * rows : (y + 1) * rows], mine, (((0,), (0,)), ((), ())), preferred_element_type=F32
        ).astype(BF)
        for h in range(h_n):
            for x in range(x_n):
                start = (h * x_n + x) * chunk
                for k in range(half // LANES):
                    to = (k * h_n + h) * chunk
                    part_ref[y * x_n + x, to : to + chunk, :] = product[
                        start : start + chunk, k * LANES : (k + 1) * LANES
                    ]


def plane_kernel(dims, part_ref, out_ref, spread):
    y_n, h_n, x_n, l_n, c_n, two = dims
    count, total_rows = part_ref.shape[0], part_ref.shape[1]
    main = total_rows - TAIL
    spread[...] = jnp.zeros_like(spread)
    group = out_ref.shape[0] // (h_n * l_n)
    lines = main // (h_n * l_n)

    def summed(start, size):
        total = part_ref[0, start : start + size, :].astype(F32)
        for p in range(1, count):
            total = total + part_ref[p, start : start + size, :].astype(F32)
        return total

    pair = lines // LINE_ROWS
    size = h_n * LINE_ROWS * l_n
    for k in range(pair):
        total = summed(k * size, size)
        for h in range(h_n):
            for r in range(LINE_ROWS):
                at = (h * LINE_ROWS + r) * l_n
                spread[pl.ds(h * l_n * group + k * LINE_ROWS + r, l_n, stride=group), :] = total[at : at + l_n]
    tail = summed(main, TAIL)
    bias = tail[0:1] + tail[1:2]
    high = bias.astype(BF).astype(F32)
    for r, value in enumerate((high, bias - high)):
        full = jnp.broadcast_to(value, (h_n * l_n, LANES))
        spread[pl.ds(lines + r, h_n * l_n, stride=group), :] = full
    out_ref[...] = spread[...].astype(BF)


def line_kernel(lines, part_ref, back_ref, out_ref):
    total = part_ref[0].astype(F32)
    for p in range(1, part_ref.shape[0]):
        total = total + part_ref[p].astype(F32)
    group = total.shape[0]
    row = iota((group, LANES), 0)
    bias = total[lines : lines + 1] + total[lines + 1 : lines + 2]
    high = bias.astype(BF).astype(F32)
    total = jnp.where(row == lines, high, jnp.where(row == lines + 1, bias - high, total))
    for p in range(out_ref.shape[0]):
        value = back_ref[p : p + 1, :]
        head = value.astype(BF).astype(F32)
        tile = jnp.where(row == group - 2, head, jnp.where(row == group - 1, value - head, total))
        out_ref[p] = tile.astype(BF)


def unpack_kernel(dims, high_ref, own_ref, both_ref, order_ref, cos_ref, weight_ref, bias_ref, wide, narrow):
    y_n, h_n, x_n, l_n, c_n, two = dims
    near, per = x_n * l_n, c_n * two
    group = own_ref.shape[0] // near
    wide[...] = both_ref[...].astype(F32)
    narrow[...] = own_ref[...].astype(F32)
    half = weight_ref.shape[1] // c_n
    pairs = half // LANES
    lines = pairs * LINE_ROWS
    for c in range(c_n):
        for x in range(x_n):
            for k in range(pairs):
                for r in range(LINE_ROWS):
                    start = (c * near + x * l_n) * group + k * LINE_ROWS + r
                    to = (x * LINE_ROWS + r) * l_n
                    at = c * half + k * LANES
                    weight_ref[to : to + l_n, at : at + LANES] = wide[pl.ds(start, l_n, stride=group), :]
    cosines = narrow[pl.ds(group - 2, near, stride=group), :] + narrow[pl.ds(group - 1, near, stride=group), :]
    order = order_ref[...]
    tokens = order.shape[1]
    base = iota((near, tokens), 0) * per
    total = jnp.zeros((near, tokens), F32)
    for i in range(per):
        total = total + jnp.where(order == base + i, cosines[:, i : i + 1], 0.0)
    cos_ref[...] = jnp.sum(total, axis=0, keepdims=True)
    cols = bias_ref.shape[1]
    blocks = cols * h_n // LANES
    offset = high_ref[0] * cols
    out = jnp.zeros((8, cols), F32)
    for b in range(blocks):
        start = b * l_n * group + lines
        pick = iota((LANES, cols), 0) + b * LANES == iota((LANES, cols), 1) + offset
        pick = jnp.where(pick, 1.0, 0.0).astype(BF)
        for r in range(2):
            term = jnp.broadcast_to(narrow[start + r : start + r + 1, :], (8, LANES)).astype(BF)
            out = out + jnp.dot(term, pick, preferred_element_type=F32)
    bias_ref[...] = out[0:1]


def local(hidden, weight, bias, patches, slots, order, cotangent):
    y_n, h_n, x_n, l_n, c_n = (lax.axis_size(a) for a in ("y", "h", "x", "l", "c"))
    patches, slots = patches[0], slots[0]
    tokens, units = hidden.shape[1:]
    width = weight.shape[1]
    patch_count = patches.shape[0]
    near = x_n * l_n
    per = tokens // near
    shards = near * c_n
    two = tokens // shards
    block = patch_count // shards
    half = width // c_n
    dims = (y_n, h_n, x_n, l_n, c_n, two)
    shape = jax.ShapeDtypeStruct
    core = lax.axis_index("c").astype(I32)[None]
    high = lax.axis_index("h").astype(I32)[None]

    sent = call(send_kernel, shape((tokens, units + LANES), BF), [VMEM] * 3)(hidden[0], order, cotangent)
    moved = lax.all_to_all(sent.reshape(near, per, units + LANES), ("x", "l"), 0, 0, tiled=True)

    at = jnp.arange(tokens, dtype=I32)
    src_core, src_chip, level = at // (near * two), (at // two) % near, at % two
    src = src_chip * c_n + src_core
    q = jnp.arange(patch_count, dtype=I32)
    match = (q[None, :] // block == src[:, None]) & (slots[None, :] == level[:, None])
    totals = jnp.dot(match.astype(BF), patches, preferred_element_type=F32)
    counts = jnp.sum(match.astype(F32), axis=1)
    pooled = lax.all_gather((totals / counts[:, None]).astype(BF), "c", axis=0, tiled=True)

    both = lax.all_gather(moved.reshape(tokens, units + LANES), "c", axis=0, tiled=True)
    rows = units // (y_n * x_n)
    lines = half // LANES * LINE_ROWS
    part, back = call(
        functools.partial(middle_kernel, dims),
        (
            shape((y_n * x_n, rows * half // LANES + TAIL, LANES), BF),
            shape((near, LANES), F32),
        ),
        [SMEM] + [VMEM] * 4,
        [
            pltpu.VMEM((c_n * tokens, width), F32),
            pltpu.VMEM((c_n * tokens, width), F32),
            pltpu.VMEM((c_n, c_n * tokens, half), BF),
        ],
    )(core, both, pooled, weight, bias[None, :])

    part = lax.all_to_all(part, ("y", "x"), 0, 0, tiled=True)
    spots = h_n * l_n
    part = call(
        functools.partial(plane_kernel, dims),
        shape((spots * TAIL, LANES), BF),
        [VMEM],
        [pltpu.VMEM((spots * TAIL, LANES), F32)],
    )(part)
    part, back = lax.optimization_barrier((part, back))
    part = lax.all_to_all(part.reshape(spots, TAIL, LANES), ("h", "l"), 0, 0, tiled=True)
    part = call(functools.partial(line_kernel, lines), shape((near, TAIL, LANES), BF), [VMEM] * 2)(part, back)
    part = lax.all_to_all(part, ("x", "l"), 0, 0, tiled=True).reshape(near * TAIL, LANES)
    wide = lax.all_gather(part, "c", axis=0, tiled=True)
    cos_sim, weight_grad, bias_grad = call(
        functools.partial(unpack_kernel, dims),
        (
            shape((1, tokens), F32),
            shape((units // (y_n * h_n), width), F32),
            shape((1, width // (y_n * h_n)), F32),
        ),
        [SMEM] + [VMEM] * 3,
        [pltpu.VMEM((c_n * near * TAIL, LANES), F32), pltpu.VMEM((near * TAIL, LANES), F32)],
    )(high, part, wide, order)
    return cos_sim, weight_grad, bias_grad[0]


def solution(mesh, sizes=(4, 4, 4, 8, 2)):
    fine = Mesh(mesh.devices.reshape(sizes), ("y", "h", "x", "l", "c"))
    clip, seq = ("y", "h"), ("x", "l", "c")
    placed = (
        P(clip, seq, None),
        P(),
        P(),
        P(clip, seq, None),
        P(clip, seq),
        P(clip, seq),
        P(clip, seq),
    )
    return jax.shard_map(
        local,
        mesh=fine,
        in_specs=placed,
        out_specs=(P(clip, seq), P(clip, None), P(clip)),
        check_vma=False,
    )
```

time: 159 us -> 149 us (0.937)
  blocking collectives: 43 us -> 89.6 us
  starting transfers between devices: 41 us -> 21 us
  waiting for transfers between devices: 41.8 us -> 27.1 us
  local copies, waits for them, and re-layouts: 15.4 us -> 5.11 us
  other arithmetic: 8.37 us -> 0.19 us
  matrix products: 7.25 us -> 0.31 us
  Pallas kernels: 0 us -> 4.68 us
    all_to_all x0 -> x1, blocking collectives: none -> 48.5 us  [local(): lax.all_to_all(part.reshape(spots, TAIL, LANES), ('h', 'l'), 0, 0, tiled=...]
    all_to_all x3 -> x2, starting transfers between devices: 41 us -> 21 us  [the longest x1 15.9 us: local(): lax.all_to_all(sent.reshape(near, per, units + LANES), ('x', 'l'), 0, 0,...]
    all_to_all x3 -> x2, waiting for transfers between devices: 41.8 us -> 27.1 us  [the longest x1 15.3 us: local(): lax.all_to_all(sent.reshape(near, per, units + LANES), ('x', 'l'), 0, 0,...]
    convert_element_type x3 -> x0, local copies, waits for them, and re-layouts: 8.8 us -> none  [local(): target = target.reshape(c_n * tokens, width).astype(F32)]
    dot_general x3 -> x0, matrix products: 5.79 us -> none  [the longest x1 2.82 us: local(): projected = jnp.dot(acts, weight, preferred_element_type=F32) + bias]
    pallas_call x0 -> x5, Pallas kernels: none -> 4.68 us  [the longest x1 2.52 us: local(): call(functools.partial(middle_kernel, dims), (shape((y_n * x_n, rows * ha...]
    reduce_sum x7 -> x0, other arithmetic: 4.5 us -> none  [the longest x1 1.37 us: local(): inv_target = lax.rsqrt(jnp.sum(target * target, axis=1) + 1e-06)]
    unnamed x12 -> x16, local copies, waits for them, and re-layouts: 0.23 us -> 4.24 us
  transfers between devices with their start and end apart: 3 -> 2, of which waited for: 3 -> 2; matrix products, arithmetic and copies ran while one was open for 9% -> 0% of each run, Pallas kernels for 0% -> 0%
where the time goes in v2:
time: 149 us
  blocking collectives  89.6 us (60%)
  waiting for transfers between devices  27.1 us (18%)
  starting transfers between devices  21 us (14%)
  local copies, waits for them, and re-layouts  5.11 us (3%)
  Pallas kernels  4.68 us (3%)
    all_to_all x1, blocking collectives, local(): lax.all_to_all(part.reshape(spots, TAIL, LANES), ('h', 'l'), 0, 0, tiled=...  48.5 us
    all_to_all x1, blocking collectives, local(): part = lax.all_to_all(part, ('y', 'x'), 0, 0, tiled=True)  27 us
    all_to_all x1, starting transfers between devices, local(): lax.all_to_all(sent.reshape(near, per, units + LANES), ('x', 'l'), 0, 0,...  15.9 us
    all_to_all x1, waiting for transfers between devices, local(): lax.all_to_all(sent.reshape(near, per, units + LANES), ('x', 'l'), 0, 0,...  15.3 us
    all_to_all x1, waiting for transfers between devices, local(): lax.all_to_all(part, ('x', 'l'), 0, 0, tiled=True)  11.8 us
    all_gather x1, blocking collectives, local(): wide = lax.all_gather(part, 'c', axis=0, tiled=True)  6.28 us
    all_to_all x1, starting transfers between devices, local(): lax.all_to_all(part, ('x', 'l'), 0, 0, tiled=True)  5.03 us
    unnamed x16, local copies, waits for them, and re-layouts  4.24 us
  transfers between devices with their start and end apart: 2, of which 2 were waited for; matrix products, arithmetic and copies ran while one was open for 0% of the time, Pallas kernels for 0%

profile of v2, /device:TPU:1, one launch (start us, length us, event | category | flops | bytes accessed | tf_op | source)
XLA Modules:
  0.0 148.7 jit_solution(8993314240733959190)
XLA Ops:
  0.6 0.0 copy-start
  0.6 0.0 copy-start.7
  0.7 0.0 copy-start.2
  0.7 1.0 copy-done.2
  1.7 0.0 copy-start.3
  1.7 0.7 copy-done.3
  2.3 0.0 copy-start.5
  2.3 0.7 copy-done.5
  3.0 0.0 copy-start.6
  3.0 0.2 shard_map.94
  3.2 0.8 reshape.99
  4.0 15.9 %all-to-all-start = ((bf16[32,4,1152]{2,1,0:T(4,128)(2,1)}), bf16[32,4,1152]{2,1,0:T(4,128)(2,1)S(1)}, u32[]{:S(2)}, u32[]{:S(2)}) async-start(bf16[32,4,1152]{2,1,0:T(4,128)(2,1)} %reshape.99), calls=%async_computation | async-start | bytes 589824 | tf_op jit(solution)/shard_map/all_to_all | solution.py:243
  19.9 0.0 copy-done.6
  20.0 0.0 copy-done.7
  20.0 0.2 convert_reduce_fusion
  20.2 0.0 copy-done
  20.2 0.3 fusion
  20.5 4.1 %all_gather.10.pooled_ref = bf16[256,1536]{1,0:T(8,128)(2,1)S(1)} all-gather(bf16[128,1536]{1,0:T(8,128)(2,1)S(1)} %fusion), channel_id=1, replica_groups=mesh['y'=4,'h'=4,'x'=4,'l'=8,'c'=2] {'c'}, dimensions={0}, use_global_device_ids=true | all-gather | bytes 1179648 | tf_op jit(solution)/shard_map/all_gather | solution.py:252
  24.6 15.3 %all-to-all-done = bf16[32,4,1152]{2,1,0:T(4,128)(2,1)S(1)} async-done(((bf16[32,4,1152]{2,1,0:T(4,128)(2,1)}), bf16[32,4,1152]{2,1,0:T(4,128)(2,1)S(1)}, u32[]{:S(2)}, u32[]{:S(2)}) %all-to-all-start) | async-done | bytes 294944 | tf_op jit(solution)/shard_map/all_to_all | solution.py:243
  39.9 0.1 reshape.100
  40.0 3.7 %all_gather.9.both_ref = bf16[256,1152]{1,0:T(8,128)(2,1)S(1)} all-gather(bf16[128,1152]{1,0:T(8,128)(2,1)S(1)} %reshape.100), channel_id=1, replica_groups=mesh['y'=4,'h'=4,'x'=4,'l'=8,'c'=2] {'c'}, dimensions={0}, use_global_device_ids=true | all-gather | bytes 884736 | tf_op jit(solution)/shard_map/all_gather | solution.py:254
  43.7 0.0 copy-start.1
  43.7 1.9 %copy-done.1 = bf16[1024,1536]{1,0:T(8,128)(2,1)S(1)} copy-done((bf16[1024,1536]{1,0:T(8,128)(2,1)S(1)}, bf16[1024,1536]{1,0:T(8,128)(2,1)}, u32[]{:S(2)}) %copy-start.1) | copy-done | bytes 3145752
  45.6 2.5 %shard_map.95 = (bf16[16,400,128]{2,1,0:T(8,128)(2,1)S(1)}, f32[32,128]{1,0:T(8,128)S(1)}) custom-call(s32[1]{0:T(128)} %bitcast.1.core_ref, bf16[256,1152]{1,0:T(8,128)(2,1)S(1)} %all_gather.9.both_ref, bf16[256,1536]{1,0:T(8,128)(2,1)S(1)} %all_gather.10.pooled_ref, bf16[1024,1536]{1,0:T(8,128)(2,1)S(1)} %copy-done.1, f32[1,1536]{1,0:T(1,128)S(1)} %broadcast_in_dim.15.bias_ref), custom_call_target="tpu_custom_call" | custom-call | tf_op jit(solution)/shard_map/pallas_call | solution.py:257
  48.1 27.0 %all_to_all.20.part_ref = bf16[16,400,128]{2,1,0:T(8,128)(2,1)S(1)} all-to-all(bf16[16,400,128]{2,1,0:T(8,128)(2,1)S(1)} %get-tuple-element.10), channel_id=1, replica_groups=mesh['y'=4,'h'=4,'x'=4,'l'=8,'c'=2] {'y','x'}, dimensions={0} | all-to-all | bytes 3276800 | tf_op jit(solution)/shard_map/all_to_all | solution.py:271
  75.1 0.0 copy-start.4
  75.1 0.3 shard_map.96
  75.4 48.5 %all_to_all.21.part_ref = bf16[32,16,128]{2,1,0:T(8,128)(2,1)S(1)} all-to-all(bf16[32,16,128]{2,1,0:T(8,128)(2,1)S(1)} %bitcast.12), channel_id=1, replica_groups=mesh['y'=4,'h'=4,'x'=4,'l'=8,'c'=2] {'h','l'}, dimensions={0} | all-to-all | bytes 262144 | tf_op jit(solution)/shard_map/all_to_all | solution.py:280
  123.9 0.7 shard_map.97
  124.6 5.0 %all-to-all-start.3 = ((bf16[32,16,128]{2,1,0:T(8,128)(2,1)}), bf16[32,16,128]{2,1,0:T(8,128)(2,1)S(1)}, u32[]{:S(2)}, u32[]{:S(2)}) async-start(bf16[32,16,128]{2,1,0:T(8,128)(2,1)} %shard_map.97), calls=%async_computation.3 | async-start | bytes 262144 | tf_op jit(solution)/shard_map/all_to_all | solution.py:282
  129.6 11.8 %all-to-all-done.3 = bf16[32,16,128]{2,1,0:T(8,128)(2,1)S(1)} async-done(((bf16[32,16,128]{2,1,0:T(8,128)(2,1)}), bf16[32,16,128]{2,1,0:T(8,128)(2,1)S(1)}, u32[]{:S(2)}, u32[]{:S(2)}) %all-to-all-start.3) | async-done | bytes 131104 | tf_op jit(solution)/shard_map/all_to_all | solution.py:282
  141.4 6.3 %all_gather.11.both_ref = bf16[1024,128]{1,0:T(8,128)(2,1)S(1)} all-gather(bf16[512,128]{1,0:T(8,128)(2,1)S(1)} %bitcast.10), channel_id=1, replica_groups=mesh['y'=4,'h'=4,'x'=4,'l'=8,'c'=2] {'c'}, dimensions={0}, use_global_device_ids=true | all-gather | bytes 393216 | tf_op jit(solution)/shard_map/all_gather | solution.py:283
  147.7 0.0 copy-done.4
  147.7 1.0 shard_map.98
  (3 shorter events, 0.0 us)
Async XLA Ops:
  0.6 19.6 %copy-start = (bf16[1,256,1536]{2,1,0:T(8,128)(2,1)S(1)}, bf16[1,256,1536]{2,1,0:T(8,128)(2,1)}, u32[]{:S(2)}) copy-start(bf16[1,256,1536]{2,1,0:T(8,128)(2,1)} %param.10) | copy-start | bytes 2359300
  0.6 19.3 %copy-start.7 = (s32[1,256]{1,0:T(1,128)S(1)}, s32[1,256]{1,0:T(1,128)}, u32[]{:S(2)}) copy-start(s32[1,256]{1,0:T(1,128)} %param.11) | copy-start | bytes 3076
  0.7 1.0 copy-start.2
  1.7 0.7 copy-start.3
  2.3 0.7 copy-start.5
  3.0 17.0 %copy-start.6 = (f32[1536]{0:T(1024)S(1)}, f32[1536]{0:T(1024)}, u32[]{:S(2)}) copy-start(f32[1536]{0:T(1024)} %param.9) | copy-start | bytes 18436
  4.0 35.9 %all-to-all-start = ((bf16[32,4,1152]{2,1,0:T(4,128)(2,1)}), bf16[32,4,1152]{2,1,0:T(4,128)(2,1)S(1)}, u32[]{:S(2)}, u32[]{:S(2)}) async-start(bf16[32,4,1152]{2,1,0:T(4,128)(2,1)} %reshape.99), calls=%async_computation | async-start | bytes 589824 | tf_op jit(solution)/shard_map/all_to_all | solution.py:243
  43.7 1.9 %copy-start.1 = (bf16[1024,1536]{1,0:T(8,128)(2,1)S(1)}, bf16[1024,1536]{1,0:T(8,128)(2,1)}, u32[]{:S(2)}) copy-start(bf16[1024,1536]{1,0:T(8,128)(2,1)} %weight_ref.1) | copy-start | bytes 9437188
  75.1 72.6 %copy-start.4 = (s32[1,128]{1,0:T(1,128)S(1)}, s32[1,128]{1,0:T(1,128)}, u32[]{:S(2)}) copy-start(s32[1,128]{1,0:T(1,128)} %order_ref.3) | copy-start | bytes 1540
  124.6 16.8 %all-to-all-start.3 = ((bf16[32,16,128]{2,1,0:T(8,128)(2,1)}), bf16[32,16,128]{2,1,0:T(8,128)(2,1)S(1)}, u32[]{:S(2)}, u32[]{:S(2)}) async-start(bf16[32,16,128]{2,1,0:T(8,128)(2,1)} %shard_map.97), calls=%async_computation.3 | async-start | bytes 262144 | tf_op jit(solution)/shard_map/all_to_all | solution.py:282

commit v3 on v2

--- a/solution.py
+++ b/solution.py
@@ -39,11 +39,11 @@
 
 def send_kernel(hidden_ref, order_ref, cot_ref, out_ref):
     tokens, units = hidden_ref.shape
+    pieces, per = out_ref.shape[:2]
     pick = order_ref[...] == iota((tokens, tokens), 0)
     rows = jnp.dot(
         jnp.where(pick, 1.0, 0.0).astype(BF), hidden_ref[...], preferred_element_type=F32
     )
-    out_ref[:, :units] = rows.astype(BF)
     cot = jnp.sum(jnp.where(pick, cot_ref[...], 0.0), axis=1, keepdims=True)
     high = cot.astype(BF).astype(F32)
     rest = cot - high
@@ -51,11 +51,30 @@
     low = rest - middle
     lane = iota((tokens, LANES), 1)
     cols = jnp.where(lane == 0, high, jnp.where(lane == 1, middle, jnp.where(lane == 2, low, 0.0)))
-    out_ref[:, units:] = cols.astype(BF)
+    for p in range(pieces):
+        at = slice(p * per, (p + 1) * per)
+        out_ref[p] = jnp.concatenate([rows[at], cols[at]], axis=1).astype(BF)
+
+
+def pool_kernel(dims, patch_ref, slot_ref, weight_ref, pooled_ref, near_ref, sem):
+    y_n, h_n, x_n, l_n, c_n, two = dims
+    fetch = pltpu.make_async_copy(weight_ref, near_ref, sem)
+    fetch.start()
+    tokens, patches = pooled_ref.shape[0], patch_ref.shape[0]
+    shape = (tokens, patches)
+    row = iota(shape, 0)
+    near = x_n * l_n
+    src = row // two % near * c_n + row // (near * two)
+    match = (iota(shape, 1) // (patches // (near * c_n)) == src) & (slot_ref[...] == row % two)
+    match = jnp.where(match, 1.0, 0.0)
+    counts = jnp.sum(match, axis=1, keepdims=True)
+    totals = jnp.dot(match.astype(BF), patch_ref[...], preferred_element_type=F32)
+    pooled_ref[...] = (totals / counts).astype(BF)
+    fetch.wait()
 
 
 def middle_kernel(
-    dims, core_ref, both_ref, pooled_ref, weight_ref, bias_ref, part_ref, back_ref, proj, target, grads
+    dims, core_ref, high_ref, both_ref, pooled_ref, weight_ref, bias_ref, part_ref, back_ref, proj, target, grads
 ):
     y_n, h_n, x_n, l_n, c_n, two = dims
     near, per = x_n * l_n, c_n * two
@@ -118,7 +137,8 @@
     for term in (high, low):
         spread = jnp.where(spot, term.astype(F32), 0.0).astype(BF)
         back = back + jnp.dot(gather, spread, preferred_element_type=F32)
-    back_ref[...] = back
+    back_ref[:near, :] = back
+    back_ref[near:, :] = jnp.full((8, LANES), high_ref[0], I32).astype(F32)
     rows = units // y_n
     chunk = rows // h_n // x_n
     mine = grads[core]
@@ -183,7 +203,9 @@
         out_ref[p] = tile.astype(BF)
 
 
-def unpack_kernel(dims, high_ref, own_ref, both_ref, order_ref, cos_ref, weight_ref, bias_ref, wide, narrow):
+def unpack_kernel(
+    dims, back_ref, own_ref, both_ref, order_ref, cos_ref, weight_ref, bias_ref, wide, narrow
+):
     y_n, h_n, x_n, l_n, c_n, two = dims
     near, per = x_n * l_n, c_n * two
     group = own_ref.shape[0] // near
@@ -210,7 +232,7 @@
     cos_ref[...] = jnp.sum(total, axis=0, keepdims=True)
     cols = bias_ref.shape[1]
     blocks = cols * h_n // LANES
-    offset = high_ref[0] * cols
+    offset = back_ref[near:, :cols].astype(I32)[0:1] * cols
     out = jnp.zeros((8, cols), F32)
     for b in range(blocks):
         start = b * l_n * group + lines
@@ -224,32 +246,30 @@
 
 def local(hidden, weight, bias, patches, slots, order, cotangent):
     y_n, h_n, x_n, l_n, c_n = (lax.axis_size(a) for a in ("y", "h", "x", "l", "c"))
-    patches, slots = patches[0], slots[0]
+    patches = patches[0]
     tokens, units = hidden.shape[1:]
     width = weight.shape[1]
-    patch_count = patches.shape[0]
     near = x_n * l_n
     per = tokens // near
     shards = near * c_n
     two = tokens // shards
-    block = patch_count // shards
     half = width // c_n
     dims = (y_n, h_n, x_n, l_n, c_n, two)
     shape = jax.ShapeDtypeStruct
     core = lax.axis_index("c").astype(I32)[None]
     high = lax.axis_index("h").astype(I32)[None]
 
-    sent = call(send_kernel, shape((tokens, units + LANES), BF), [VMEM] * 3)(hidden[0], order, cotangent)
-    moved = lax.all_to_all(sent.reshape(near, per, units + LANES), ("x", "l"), 0, 0, tiled=True)
-
-    at = jnp.arange(tokens, dtype=I32)
-    src_core, src_chip, level = at // (near * two), (at // two) % near, at % two
-    src = src_chip * c_n + src_core
-    q = jnp.arange(patch_count, dtype=I32)
-    match = (q[None, :] // block == src[:, None]) & (slots[None, :] == level[:, None])
-    totals = jnp.dot(match.astype(BF), patches, preferred_element_type=F32)
-    counts = jnp.sum(match.astype(F32), axis=1)
-    pooled = lax.all_gather((totals / counts[:, None]).astype(BF), "c", axis=0, tiled=True)
+    sent = call(send_kernel, shape((near, per, units + LANES), BF), [VMEM] * 3, limit=60)(
+        hidden[0], order, cotangent
+    )
+    moved = lax.all_to_all(sent, ("x", "l"), 0, 0, tiled=True)
+    pooled, weight = call(
+        functools.partial(pool_kernel, dims),
+        (shape((tokens, width), BF), shape(weight.shape, BF)),
+        [VMEM, VMEM, pl.BlockSpec(memory_space=pl.ANY)],
+        [pltpu.SemaphoreType.DMA],
+    )(patches, slots, weight)
+    pooled = lax.all_gather(pooled, "c", axis=0, tiled=True)
 
     both = lax.all_gather(moved.reshape(tokens, units + LANES), "c", axis=0, tiled=True)
     rows = units // (y_n * x_n)
@@ -258,15 +278,15 @@
         functools.partial(middle_kernel, dims),
         (
             shape((y_n * x_n, rows * half // LANES + TAIL, LANES), BF),
-            shape((near, LANES), F32),
+            shape((near + 8, LANES), F32),
         ),
-        [SMEM] + [VMEM] * 4,
+        [SMEM] * 2 + [VMEM] * 4,
         [
             pltpu.VMEM((c_n * tokens, width), F32),
             pltpu.VMEM((c_n * tokens, width), F32),
             pltpu.VMEM((c_n, c_n * tokens, half), BF),
         ],
-    )(core, both, pooled, weight, bias[None, :])
+    )(core, high, both, pooled, weight, bias[None, :])
 
     part = lax.all_to_all(part, ("y", "x"), 0, 0, tiled=True)
     spots = h_n * l_n
@@ -288,9 +308,9 @@
             shape((units // (y_n * h_n), width), F32),
             shape((1, width // (y_n * h_n)), F32),
         ),
-        [SMEM] + [VMEM] * 3,
+        [VMEM] * 4,
         [pltpu.VMEM((c_n * near * TAIL, LANES), F32), pltpu.VMEM((near * TAIL, LANES), F32)],
-    )(high, part, wide, order)
+    )(back, part, wide, order)
     return cos_sim, weight_grad, bias_grad[0]
 
 

time: 149 us -> 147 us (0.987)
  blocking collectives: 89.6 us -> 107 us
  waiting for transfers between devices: 27.1 us -> 10.1 us
  starting transfers between devices: 21 us -> 16 us
  Pallas kernels: 4.68 us -> 6.23 us
    all_to_all x2 -> x1, waiting for transfers between devices: 27.1 us -> 10.1 us  [local(): moved = lax.all_to_all(sent, ('x', 'l'), 0, 0, tiled=True)]
    all_to_all x0 -> x1, blocking collectives: none -> 16.6 us  [local(): lax.all_to_all(part, ('x', 'l'), 0, 0, tiled=True)]
    all_to_all x2 -> x1, starting transfers between devices: 21 us -> 16 us  [local(): moved = lax.all_to_all(sent, ('x', 'l'), 0, 0, tiled=True)]
    pallas_call x1 -> x2, Pallas kernels: 0.21 us -> 2.39 us  [the longest x1 1.9 us: local(): call(send_kernel, shape((near, per, units + LANES), BF), [VMEM] * 3, limi...]
    unnamed x16 -> x10, local copies, waits for them, and re-layouts: 4.24 us -> 4.84 us
  transfers between devices with their start and end apart: 2 -> 1, of which waited for: 2 -> 1; matrix products, arithmetic and copies ran while one was open for 0% -> 0% of each run, Pallas kernels for 0% -> 0%
where the time goes in v3:
time: 147 us; the launch traced here: 146 us
  blocking collectives  107 us (73%)
  starting transfers between devices  16 us (11%)
  waiting for transfers between devices  10.1 us (7%)
  local copies, waits for them, and re-layouts  6.58 us (4%)
  Pallas kernels  6.23 us (4%)
    all_to_all x1, blocking collectives, local(): lax.all_to_all(part.reshape(spots, TAIL, LANES), ('h', 'l'), 0, 0, tiled=...  48.5 us
    all_to_all x1, blocking collectives, local(): part = lax.all_to_all(part, ('y', 'x'), 0, 0, tiled=True)  27 us
    all_to_all x1, blocking collectives, local(): lax.all_to_all(part, ('x', 'l'), 0, 0, tiled=True)  16.6 us
    all_to_all x1, starting transfers between devices, local(): moved = lax.all_to_all(sent, ('x', 'l'), 0, 0, tiled=True)  16 us
    all_to_all x1, waiting for transfers between devices, local(): moved = lax.all_to_all(sent, ('x', 'l'), 0, 0, tiled=True)  10.1 us
    all_gather x1, blocking collectives, local(): wide = lax.all_gather(part, 'c', axis=0, tiled=True)  5.72 us
    unnamed x10, local copies, waits for them, and re-layouts  4.84 us
    all_gather x1, blocking collectives, local(): pooled = lax.all_gather(pooled, 'c', axis=0, tiled=True)  4.83 us
  transfers between devices with their start and end apart: 1, of which 1 were waited for; matrix products, arithmetic and copies ran while one was open for 0% of the time, Pallas kernels for 0%

profile of v3, /device:TPU:1, one launch (start us, length us, event | category | flops | bytes accessed | tf_op | source)
XLA Modules:
  0.0 146.1 jit_solution(10712809790466000793)
XLA Ops:
  0.6 1.9 %shard_map.94 = bf16[32,4,1152]{2,1,0:T(4,128)(2,1)} custom-call(bf16[128,1024]{1,0:T(8,128)(2,1)} %bitcast.11, s32[1,128]{1,0:T(1,128)} %order_ref.3, f32[1,128]{1,0:T(1,128)} %cot_ref.1), custom_call_target="tpu_custom_call" | custom-call | tf_op jit(solution)/shard_map/pallas_call | solution.py:262
  2.5 16.0 %all-to-all-start = ((bf16[32,4,1152]{2,1,0:T(4,128)(2,1)}), bf16[32,4,1152]{2,1,0:T(4,128)(2,1)}, u32[]{:S(2)}, u32[]{:S(2)}) async-start(bf16[32,4,1152]{2,1,0:T(4,128)(2,1)} %shard_map.94), calls=%async_computation | async-start | bytes 589824 | tf_op jit(solution)/shard_map/all_to_all | solution.py:265
  18.6 0.7 broadcast_in_dim.11.bias_ref
  19.3 0.0 copy-start
  19.3 1.9 %copy-done = bf16[1024,1536]{1,0:T(8,128)(2,1)S(1)} copy-done((bf16[1024,1536]{1,0:T(8,128)(2,1)S(1)}, bf16[1024,1536]{1,0:T(8,128)(2,1)}, u32[]{:S(2)}) %copy-start) | copy-done | bytes 3145752
  21.2 0.0 copy-start.2
  21.2 1.1 copy-done.2
  22.3 0.0 copy-start.4
  22.3 0.7 copy-done.4
  23.0 0.5 shard_map.95
  23.5 4.8 %all_gather.10.pooled_ref = bf16[256,1536]{1,0:T(8,128)(2,1)} all-gather(bf16[128,1536]{1,0:T(8,128)(2,1)S(1)} %get-tuple-element.12), channel_id=1, replica_groups=mesh['y'=4,'h'=4,'x'=4,'l'=8,'c'=2] {'c'}, dimensions={0}, use_global_device_ids=true | all-gather | bytes 1179648 | tf_op jit(solution)/shard_map/all_gather | solution.py:272
  28.3 10.1 %all-to-all-done = bf16[32,4,1152]{2,1,0:T(4,128)(2,1)} async-done(((bf16[32,4,1152]{2,1,0:T(4,128)(2,1)}), bf16[32,4,1152]{2,1,0:T(4,128)(2,1)}, u32[]{:S(2)}, u32[]{:S(2)}) %all-to-all-start) | async-done | bytes 294944 | tf_op jit(solution)/shard_map/all_to_all | solution.py:265
  38.4 1.0 reshape.15
  39.4 3.9 %all_gather.9.both_ref = bf16[256,1152]{1,0:T(8,128)(2,1)S(1)} all-gather(bf16[128,1152]{1,0:T(8,128)(2,1)S(1)} %reshape.15), channel_id=1, replica_groups=mesh['y'=4,'h'=4,'x'=4,'l'=8,'c'=2] {'c'}, dimensions={0}, use_global_device_ids=true | all-gather | bytes 884736 | tf_op jit(solution)/shard_map/all_gather | solution.py:274
  43.3 0.0 copy-start.1
  43.3 1.1 copy-done.1
  44.4 2.5 %shard_map.96 = (bf16[16,400,128]{2,1,0:T(8,128)(2,1)S(1)}, f32[40,128]{1,0:T(8,128)S(1)}) custom-call(s32[1]{0:T(128)} %bitcast.core_ref, s32[1]{0:T(128)} %bitcast.1.high_ref, bf16[256,1152]{1,0:T(8,128)(2,1)S(1)} %all_gather.9.both_ref, bf16[256,1536]{1,0:T(8,128)(2,1)S(1)} %copy-done.1, bf16[1024,1536]{1,0:T(8,128)(2,1)S(1)} %get-tuple-element.13.weight_ref, ...), custom_call_target="tpu_custom_call" | custom-call | tf_op jit(solution)/shard_map/pallas_call | solution.py:277
  47.0 0.0 copy-start.3
  47.0 27.0 %all_to_all.20.part_ref = bf16[16,400,128]{2,1,0:T(8,128)(2,1)S(1)} all-to-all(bf16[16,400,128]{2,1,0:T(8,128)(2,1)S(1)} %get-tuple-element.14), channel_id=1, replica_groups=mesh['y'=4,'h'=4,'x'=4,'l'=8,'c'=2] {'y','x'}, dimensions={0} | all-to-all | bytes 3276800 | tf_op jit(solution)/shard_map/all_to_all | solution.py:291
  74.0 0.3 shard_map.97
  74.2 48.5 %all_to_all.21.part_ref = bf16[32,16,128]{2,1,0:T(8,128)(2,1)S(1)} all-to-all(bf16[32,16,128]{2,1,0:T(8,128)(2,1)S(1)} %bitcast.10), channel_id=1, replica_groups=mesh['y'=4,'h'=4,'x'=4,'l'=8,'c'=2] {'h','l'}, dimensions={0} | all-to-all | bytes 262144 | tf_op jit(solution)/shard_map/all_to_all | solution.py:300
  122.7 0.1 shard_map.98
  122.8 16.6 %all_to_all.22 = bf16[32,16,128]{2,1,0:T(8,128)(2,1)S(1)} all-to-all(bf16[32,16,128]{2,1,0:T(8,128)(2,1)S(1)} %shard_map.98), channel_id=1, replica_groups=mesh['y'=4,'h'=4,'x'=4,'l'=8,'c'=2] {'x','l'}, dimensions={0} | all-to-all | bytes 262144 | tf_op jit(solution)/shard_map/all_to_all | solution.py:302
  139.4 5.7 %all_gather.11.both_ref = bf16[1024,128]{1,0:T(8,128)(2,1)S(1)} all-gather(bf16[512,128]{1,0:T(8,128)(2,1)S(1)} %bitcast.7), channel_id=1, replica_groups=mesh['y'=4,'h'=4,'x'=4,'l'=8,'c'=2] {'c'}, dimensions={0}, use_global_device_ids=true | all-gather | bytes 393216 | tf_op jit(solution)/shard_map/all_gather | solution.py:303
  145.1 0.0 copy-done.3
  145.1 1.0 shard_map.99
Async XLA Ops:
  2.5 35.8 %all-to-all-start = ((bf16[32,4,1152]{2,1,0:T(4,128)(2,1)}), bf16[32,4,1152]{2,1,0:T(4,128)(2,1)}, u32[]{:S(2)}, u32[]{:S(2)}) async-start(bf16[32,4,1152]{2,1,0:T(4,128)(2,1)} %shard_map.94), calls=%async_computation | async-start | bytes 589824 | tf_op jit(solution)/shard_map/all_to_all | solution.py:265
  19.3 1.9 %copy-start = (bf16[1024,1536]{1,0:T(8,128)(2,1)S(1)}, bf16[1024,1536]{1,0:T(8,128)(2,1)}, u32[]{:S(2)}) copy-start(bf16[1024,1536]{1,0:T(8,128)(2,1)} %weight_ref.1) | copy-start | bytes 9437188
  21.2 1.1 copy-start.2
  22.3 0.7 copy-start.4
  43.3 1.1 copy-start.1
  47.0 98.1 %copy-start.3 = (s32[1,128]{1,0:T(1,128)S(1)}, s32[1,128]{1,0:T(1,128)}, u32[]{:S(2)}) copy-start(s32[1,128]{1,0:T(1,128)} %order_ref.3) | copy-start | bytes 1540

commit v4 on v3

--- a/solution.py
+++ b/solution.py
@@ -26,7 +26,7 @@
     return head, (values - head.astype(F32)).astype(BF)
 
 
-def call(body, outs, ins, scratch=(), limit=40):
+def call(body, outs, ins, scratch=(), limit=16):
     return pl.pallas_call(
         body,
         out_shape=outs,
@@ -56,10 +56,8 @@
         out_ref[p] = jnp.concatenate([rows[at], cols[at]], axis=1).astype(BF)
 
 
-def pool_kernel(dims, patch_ref, slot_ref, weight_ref, pooled_ref, near_ref, sem):
+def pool_kernel(dims, patch_ref, slot_ref, pooled_ref):
     y_n, h_n, x_n, l_n, c_n, two = dims
-    fetch = pltpu.make_async_copy(weight_ref, near_ref, sem)
-    fetch.start()
     tokens, patches = pooled_ref.shape[0], patch_ref.shape[0]
     shape = (tokens, patches)
     row = iota(shape, 0)
@@ -70,11 +68,10 @@
     counts = jnp.sum(match, axis=1, keepdims=True)
     totals = jnp.dot(match.astype(BF), patch_ref[...], preferred_element_type=F32)
     pooled_ref[...] = (totals / counts).astype(BF)
-    fetch.wait()
 
 
 def middle_kernel(
-    dims, core_ref, high_ref, both_ref, pooled_ref, weight_ref, bias_ref, part_ref, back_ref, proj, target, grads
+    dims, core_ref, high_ref, both_ref, pooled_ref, other_ref, weight_ref, bias_ref, part_ref, back_ref, proj, target, grads
 ):
     y_n, h_n, x_n, l_n, c_n, two = dims
     near, per = x_n * l_n, c_n * two
@@ -83,11 +80,12 @@
     half = width // c_n
     single = tokens // c_n
     core = core_ref[0]
-    row = iota((tokens, tokens), 0)
-    wanted = (
-        (row // two) % c_n * single + row // single * (near * two) + row // per % near * two + row % two
-    )
-    turn = jnp.where(wanted == iota((tokens, tokens), 1), 1.0, 0.0).astype(BF)
+    row = iota((tokens, single), 0)
+    wanted = row // single * (near * two) + row // per % near * two + row % two
+    place = wanted == iota((tokens, single), 1)
+    ours = row // two % c_n == core
+    turn = jnp.where(place & ours, 1.0, 0.0).astype(BF)
+    turn_other = jnp.where(place & (row // two % c_n != core), 1.0, 0.0).astype(BF)
     acts = both_ref[:, :units]
     step = 256
     s_pp = jnp.zeros((tokens, 1), F32)
@@ -97,6 +95,7 @@
         cut = slice(at, at + step)
         p = jnp.dot(acts, weight_ref[:, cut], preferred_element_type=F32) + bias_ref[:, cut]
         t = jnp.dot(turn, pooled_ref[:, cut], preferred_element_type=F32)
+        t = t + jnp.dot(turn_other, other_ref[:, cut], preferred_element_type=F32)
         proj[:, cut] = p
         target[:, cut] = t
         s_pp = s_pp + jnp.sum(p * p, axis=1, keepdims=True)
@@ -263,13 +262,10 @@
         hidden[0], order, cotangent
     )
     moved = lax.all_to_all(sent, ("x", "l"), 0, 0, tiled=True)
-    pooled, weight = call(
-        functools.partial(pool_kernel, dims),
-        (shape((tokens, width), BF), shape(weight.shape, BF)),
-        [VMEM, VMEM, pl.BlockSpec(memory_space=pl.ANY)],
-        [pltpu.SemaphoreType.DMA],
-    )(patches, slots, weight)
-    pooled = lax.all_gather(pooled, "c", axis=0, tiled=True)
+    pooled = call(
+        functools.partial(pool_kernel, dims), shape((tokens, width), BF), [VMEM] * 2, limit=8
+    )(patches, slots)
+    other = lax.ppermute(pooled, "c", [(c, (c + 1) % c_n) for c in range(c_n)])
 
     both = lax.all_gather(moved.reshape(tokens, units + LANES), "c", axis=0, tiled=True)
     rows = units // (y_n * x_n)
@@ -280,13 +276,13 @@
             shape((y_n * x_n, rows * half // LANES + TAIL, LANES), BF),
             shape((near + 8, LANES), F32),
         ),
-        [SMEM] * 2 + [VMEM] * 4,
+        [SMEM] * 2 + [VMEM] * 5,
         [
             pltpu.VMEM((c_n * tokens, width), F32),
             pltpu.VMEM((c_n * tokens, width), F32),
             pltpu.VMEM((c_n, c_n * tokens, half), BF),
         ],
-    )(core, high, both, pooled, weight, bias[None, :])
+    )(core, high, both, pooled, other, weight, bias[None, :])
 
     part = lax.all_to_all(part, ("y", "x"), 0, 0, tiled=True)
     spots = h_n * l_n

time: 147 us -> 148 us (level)
  blocking collectives: 107 us -> 102 us
  starting transfers between devices: 16 us -> 20.9 us
  local copies, waits for them, and re-layouts: 6.58 us -> 3.57 us
  waiting for transfers between devices: 10.1 us -> 13.1 us
    all_gather x1 -> x0, blocking collectives: 4.83 us -> none  [local(): pooled = lax.all_gather(pooled, 'c', axis=0, tiled=True)]
    ppermute x0 -> x1, starting transfers between devices: none -> 4.6 us  [local(): other = lax.ppermute(pooled, 'c', [(c, (c + 1) % c_n) for c in range(c_n)])]
    unnamed x10, local copies, waits for them, and re-layouts: 4.84 us -> 1.82 us
    all_to_all x1, waiting for transfers between devices: 10.1 us -> 13.1 us  [local(): moved = lax.all_to_all(sent, ('x', 'l'), 0, 0, tiled=True)]
  transfers between devices with their start and end apart: 1 -> 2, of which waited for: 1 -> 1; matrix products, arithmetic and copies ran while one was open for 0% -> 1% of each run, Pallas kernels for 0% -> 0%
where the time goes in v4:
time: 148 us; the launch traced here: 147 us
  blocking collectives  102 us (69%)
  starting transfers between devices  20.9 us (14%)
  waiting for transfers between devices  13.1 us (9%)
  Pallas kernels  7.26 us (5%)
  local copies, waits for them, and re-layouts  3.57 us (2%)
    all_to_all x1, blocking collectives, local(): lax.all_to_all(part.reshape(spots, TAIL, LANES), ('h', 'l'), 0, 0, tiled=...  48.5 us
    all_to_all x1, blocking collectives, local(): part = lax.all_to_all(part, ('y', 'x'), 0, 0, tiled=True)  27 us
    all_to_all x1, blocking collectives, local(): lax.all_to_all(part, ('x', 'l'), 0, 0, tiled=True)  16.6 us
    all_to_all x1, starting transfers between devices, local(): moved = lax.all_to_all(sent, ('x', 'l'), 0, 0, tiled=True)  16.3 us
    all_to_all x1, waiting for transfers between devices, local(): moved = lax.all_to_all(sent, ('x', 'l'), 0, 0, tiled=True)  13.1 us
    all_gather x1, blocking collectives, local(): wide = lax.all_gather(part, 'c', axis=0, tiled=True)  5.73 us
    ppermute x1, starting transfers between devices, local(): other = lax.ppermute(pooled, 'c', [(c, (c + 1) % c_n) for c in range(c_n)])  4.6 us
    all_gather x1, blocking collectives, local(): lax.all_gather(moved.reshape(tokens, units + LANES), 'c', axis=0, tiled=T...  4.1 us
  transfers between devices with their start and end apart: 2, of which 1 were waited for; matrix products, arithmetic and copies ran while one was open for 1% of the time, Pallas kernels for 0%

profile of v4, /device:TPU:1, one launch (start us, length us, event | category | flops | bytes accessed | tf_op | source)
XLA Modules:
  0.0 147.4 jit_solution(7103697503928305537)
XLA Ops:
  0.6 0.0 copy-start.4
  0.6 1.9 %shard_map.94 = bf16[32,4,1152]{2,1,0:T(4,128)(2,1)} custom-call(bf16[128,1024]{1,0:T(8,128)(2,1)} %bitcast.11, s32[1,128]{1,0:T(1,128)} %order_ref.3, f32[1,128]{1,0:T(1,128)} %cot_ref.1), custom_call_target="tpu_custom_call" | custom-call | tf_op jit(solution)/shard_map/pallas_call | solution.py:261
  2.5 0.0 copy-start
  2.5 16.3 %all-to-all-start = ((bf16[32,4,1152]{2,1,0:T(4,128)(2,1)}), bf16[32,4,1152]{2,1,0:T(4,128)(2,1)}, u32[]{:S(2)}, u32[]{:S(2)}) async-start(bf16[32,4,1152]{2,1,0:T(4,128)(2,1)} %shard_map.94), calls=%async_computation | async-start | bytes 589824 | tf_op jit(solution)/shard_map/all_to_all | solution.py:264
  18.9 0.0 copy-start.1
  18.9 1.1 copy-done.1
  20.0 0.0 copy-start.3
  20.0 0.7 copy-done.3
  20.7 0.3 shard_map.95.pooled_ref
  21.0 4.6 %collective-permute-start = (bf16[128,1536]{1,0:T(8,128)(2,1)S(1)}, bf16[128,1536]{1,0:T(8,128)(2,1)}, u32[]{:S(2)}, u32[]{:S(2)}) collective-permute-start(bf16[128,1536]{1,0:T(8,128)(2,1)S(1)} %shard_map.95.pooled_ref), channel_id=1, source_target_pairs={{0,1},{1,0},{2,3},{3,2},{4,5},{5,4},{6,7},{7,6},{8,9},{9,8},{10,11... | collective-permute-start | bytes 1179656 | tf_op jit(solution)/shard_map/ppermute | solution.py:268
  25.6 0.0 copy-done.4
  25.6 13.1 %all-to-all-done = bf16[32,4,1152]{2,1,0:T(4,128)(2,1)} async-done(((bf16[32,4,1152]{2,1,0:T(4,128)(2,1)}), bf16[32,4,1152]{2,1,0:T(4,128)(2,1)}, u32[]{:S(2)}, u32[]{:S(2)}) %all-to-all-start) | async-done | bytes 294944 | tf_op jit(solution)/shard_map/all_to_all | solution.py:264
  38.7 1.7 %reshape.15 = bf16[128,1152]{1,0:T(8,128)(2,1)} reshape(bf16[32,4,1152]{2,1,0:T(4,128)(2,1)} %all-to-all-done) | data formatting | bytes 589824 | tf_op jit(solution)/shard_map/reshape | solution.py:270
  40.4 4.1 %all_gather.6.both_ref = bf16[256,1152]{1,0:T(8,128)(2,1)S(1)} all-gather(bf16[128,1152]{1,0:T(8,128)(2,1)} %reshape.15), channel_id=1, replica_groups=mesh['y'=4,'h'=4,'x'=4,'l'=8,'c'=2] {'c'}, dimensions={0}, use_global_device_ids=true | all-gather | bytes 884736 | tf_op jit(solution)/shard_map/all_gather | solution.py:270
  44.5 0.0 collective-permute-done.other_ref
  44.5 0.0 copy-done
  44.5 3.8 %shard_map.96 = (bf16[16,400,128]{2,1,0:T(8,128)(2,1)S(1)}, f32[40,128]{1,0:T(8,128)S(1)}) custom-call(s32[1]{0:T(128)} %bitcast.core_ref, s32[1]{0:T(128)} %bitcast.1.high_ref, bf16[256,1152]{1,0:T(8,128)(2,1)S(1)} %all_gather.6.both_ref, bf16[128,1536]{1,0:T(8,128)(2,1)S(1)} %shard_map.95.pooled_ref, bf16[128,1536]{1,0:T(8,128)(2,1)} %collective-permute-done.other_ref, ...), custom_call_target="tpu_custom_call" | custom-call | tf_op jit(solution)/shard_map/pallas_call | solution.py:273
  48.3 27.0 %all_to_all.20.part_ref = bf16[16,400,128]{2,1,0:T(8,128)(2,1)S(1)} all-to-all(bf16[16,400,128]{2,1,0:T(8,128)(2,1)S(1)} %get-tuple-element.10), channel_id=1, replica_groups=mesh['y'=4,'h'=4,'x'=4,'l'=8,'c'=2] {'y','x'}, dimensions={0} | all-to-all | bytes 3276800 | tf_op jit(solution)/shard_map/all_to_all | solution.py:287
  75.3 0.0 copy-start.2
  75.3 0.3 shard_map.97
  75.6 48.5 %all_to_all.21.part_ref = bf16[32,16,128]{2,1,0:T(8,128)(2,1)S(1)} all-to-all(bf16[32,16,128]{2,1,0:T(8,128)(2,1)S(1)} %bitcast.10), channel_id=1, replica_groups=mesh['y'=4,'h'=4,'x'=4,'l'=8,'c'=2] {'h','l'}, dimensions={0} | all-to-all | bytes 262144 | tf_op jit(solution)/shard_map/all_to_all | solution.py:296
  124.0 0.1 shard_map.98
  124.1 16.6 %all_to_all.22 = bf16[32,16,128]{2,1,0:T(8,128)(2,1)S(1)} all-to-all(bf16[32,16,128]{2,1,0:T(8,128)(2,1)S(1)} %shard_map.98), channel_id=1, replica_groups=mesh['y'=4,'h'=4,'x'=4,'l'=8,'c'=2] {'x','l'}, dimensions={0} | all-to-all | bytes 262144 | tf_op jit(solution)/shard_map/all_to_all | solution.py:298
  140.7 5.7 %all_gather.7.both_ref = bf16[1024,128]{1,0:T(8,128)(2,1)S(1)} all-gather(bf16[512,128]{1,0:T(8,128)(2,1)S(1)} %bitcast.7), channel_id=1, replica_groups=mesh['y'=4,'h'=4,'x'=4,'l'=8,'c'=2] {'c'}, dimensions={0}, use_global_device_ids=true | all-gather | bytes 393216 | tf_op jit(solution)/shard_map/all_gather | solution.py:299
  146.4 0.0 copy-done.2
  146.4 1.0 shard_map.99
  (1 shorter events, 0.0 us)
Async XLA Ops:
  0.6 24.9 %copy-start.4 = (f32[1536]{0:T(1024)S(1)}, f32[1536]{0:T(1024)}, u32[]{:S(2)}) copy-start(f32[1536]{0:T(1024)} %param.9) | copy-start | bytes 18436
  2.5 42.0 %copy-start = (bf16[1024,1536]{1,0:T(8,128)(2,1)S(1)}, bf16[1024,1536]{1,0:T(8,128)(2,1)}, u32[]{:S(2)}) copy-start(bf16[1024,1536]{1,0:T(8,128)(2,1)} %weight_ref.1) | copy-start | bytes 9437188
  2.5 36.1 %all-to-all-start = ((bf16[32,4,1152]{2,1,0:T(4,128)(2,1)}), bf16[32,4,1152]{2,1,0:T(4,128)(2,1)}, u32[]{:S(2)}, u32[]{:S(2)}) async-start(bf16[32,4,1152]{2,1,0:T(4,128)(2,1)} %shard_map.94), calls=%async_computation | async-start | bytes 589824 | tf_op jit(solution)/shard_map/all_to_all | solution.py:264
  18.9 1.1 copy-start.1
  20.0 0.7 copy-start.3
  21.0 23.6 %collective-permute-start = (bf16[128,1536]{1,0:T(8,128)(2,1)S(1)}, bf16[128,1536]{1,0:T(8,128)(2,1)}, u32[]{:S(2)}, u32[]{:S(2)}) collective-permute-start(bf16[128,1536]{1,0:T(8,128)(2,1)S(1)} %shard_map.95.pooled_ref), channel_id=1, source_target_pairs={{0,1},{1,0},{2,3},{3,2},{4,5},{5,4},{6,7},{7,6},{8,9},{9,8},{10,11... | collective-permute-start | bytes 1179656 | tf_op jit(solution)/shard_map/ppermute | solution.py:268
  75.3 71.1 %copy-start.2 = (s32[1,128]{1,0:T(1,128)S(1)}, s32[1,128]{1,0:T(1,128)}, u32[]{:S(2)}) copy-start(s32[1,128]{1,0:T(1,128)} %order_ref.3) | copy-start | bytes 1540

commit v5 on v3

--- a/solution.py
+++ b/solution.py
@@ -26,7 +26,7 @@
     return head, (values - head.astype(F32)).astype(BF)
 
 
-def call(body, outs, ins, scratch=(), limit=40):
+def call(body, outs, ins, scratch=(), limit=16):
     return pl.pallas_call(
         body,
         out_shape=outs,
@@ -56,25 +56,9 @@
         out_ref[p] = jnp.concatenate([rows[at], cols[at]], axis=1).astype(BF)
 
 
-def pool_kernel(dims, patch_ref, slot_ref, weight_ref, pooled_ref, near_ref, sem):
-    y_n, h_n, x_n, l_n, c_n, two = dims
-    fetch = pltpu.make_async_copy(weight_ref, near_ref, sem)
-    fetch.start()
-    tokens, patches = pooled_ref.shape[0], patch_ref.shape[0]
-    shape = (tokens, patches)
-    row = iota(shape, 0)
-    near = x_n * l_n
-    src = row // two % near * c_n + row // (near * two)
-    match = (iota(shape, 1) // (patches // (near * c_n)) == src) & (slot_ref[...] == row % two)
-    match = jnp.where(match, 1.0, 0.0)
-    counts = jnp.sum(match, axis=1, keepdims=True)
-    totals = jnp.dot(match.astype(BF), patch_ref[...], preferred_element_type=F32)
-    pooled_ref[...] = (totals / counts).astype(BF)
-    fetch.wait()
-
-
 def middle_kernel(
-    dims, core_ref, high_ref, both_ref, pooled_ref, weight_ref, bias_ref, part_ref, back_ref, proj, target, grads
+    dims, core_ref, high_ref, both_ref, pooled_ref, weight_ref, bias_ref, part_ref, back_ref,
+    proj, target, grads, held, sems
 ):
     y_n, h_n, x_n, l_n, c_n, two = dims
     near, per = x_n * l_n, c_n * two
@@ -83,6 +67,11 @@
     half = width // c_n
     single = tokens // c_n
     core = core_ref[0]
+    fetch = []
+    for k in range(sems.shape[0]):
+        cut = pl.ds(k * (width // sems.shape[0]), width // sems.shape[0])
+        fetch.append(pltpu.make_async_copy(weight_ref.at[:, cut], held.at[:, cut], sems.at[k]))
+        fetch[-1].start()
     row = iota((tokens, tokens), 0)
     wanted = (
         (row // two) % c_n * single + row // single * (near * two) + row // per % near * two + row % two
@@ -95,13 +84,16 @@
     s_pt = jnp.zeros((tokens, 1), F32)
     for at in range(0, width, step):
         cut = slice(at, at + step)
-        p = jnp.dot(acts, weight_ref[:, cut], preferred_element_type=F32) + bias_ref[:, cut]
         t = jnp.dot(turn, pooled_ref[:, cut], preferred_element_type=F32)
+        target[:, cut] = t
+        s_tt = s_tt + jnp.sum(t * t, axis=1, keepdims=True)
+    for at in range(0, width, step):
+        cut = slice(at, at + step)
+        fetch[at // step].wait()
+        p = jnp.dot(acts, held[:, cut], preferred_element_type=F32) + bias_ref[:, cut]
         proj[:, cut] = p
-        target[:, cut] = t
         s_pp = s_pp + jnp.sum(p * p, axis=1, keepdims=True)
-        s_tt = s_tt + jnp.sum(t * t, axis=1, keepdims=True)
-        s_pt = s_pt + jnp.sum(p * t, axis=1, keepdims=True)
+        s_pt = s_pt + jnp.sum(p * target[:, cut], axis=1, keepdims=True)
     inv_proj = lax.rsqrt(s_pp + 1e-06)
     inv_target = lax.rsqrt(s_tt + 1e-06)
     cosine = s_pt * inv_proj * inv_target
@@ -263,12 +255,13 @@
         hidden[0], order, cotangent
     )
     moved = lax.all_to_all(sent, ("x", "l"), 0, 0, tiled=True)
-    pooled, weight = call(
-        functools.partial(pool_kernel, dims),
-        (shape((tokens, width), BF), shape(weight.shape, BF)),
-        [VMEM, VMEM, pl.BlockSpec(memory_space=pl.ANY)],
-        [pltpu.SemaphoreType.DMA],
-    )(patches, slots, weight)
+    at = jnp.arange(tokens, dtype=I32)
+    src = (at // two) % near * c_n + at // (near * two)
+    block = patches.shape[0] // (near * c_n)
+    q = jnp.arange(patches.shape[0], dtype=I32)
+    match = (q[None, :] // block == src[:, None]) & (slots[0][None, :] == (at % two)[:, None])
+    totals = jnp.dot(match.astype(BF), patches, preferred_element_type=F32)
+    pooled = (totals / jnp.sum(match.astype(F32), axis=1)[:, None]).astype(BF)
     pooled = lax.all_gather(pooled, "c", axis=0, tiled=True)
 
     both = lax.all_gather(moved.reshape(tokens, units + LANES), "c", axis=0, tiled=True)
@@ -280,12 +273,15 @@
             shape((y_n * x_n, rows * half // LANES + TAIL, LANES), BF),
             shape((near + 8, LANES), F32),
         ),
-        [SMEM] * 2 + [VMEM] * 4,
+        [SMEM] * 2 + [VMEM] * 2 + [pl.BlockSpec(memory_space=pl.ANY), VMEM],
         [
             pltpu.VMEM((c_n * tokens, width), F32),
             pltpu.VMEM((c_n * tokens, width), F32),
             pltpu.VMEM((c_n, c_n * tokens, half), BF),
+            pltpu.VMEM((units, width), BF),
+            pltpu.SemaphoreType.DMA((width // 256,)),
         ],
+        limit=50,
     )(core, high, both, pooled, weight, bias[None, :])
 
     part = lax.all_to_all(part, ("y", "x"), 0, 0, tiled=True)

time: 147 us -> 147 us (level)
  local copies, waits for them, and re-layouts: 6.58 us -> 0.79 us
  waiting for transfers between devices: 10.1 us -> 13.3 us
  Pallas kernels: 6.23 us -> 8.65 us
    unnamed x10 -> x4, local copies, waits for them, and re-layouts: 4.84 us -> 0.01 us
    all_to_all x1, waiting for transfers between devices: 10.1 us -> 13.3 us  [local(): moved = lax.all_to_all(sent, ('x', 'l'), 0, 0, tiled=True)]
    pallas_call x1, Pallas kernels: 2.53 us -> 5.37 us  [local(): call(functools.partial(middle_kernel, dims), (shape((y_n * x_n, rows * ha...]
  transfers between devices with their start and end apart: 1 -> 1, of which waited for: 1 -> 1; matrix products, arithmetic and copies ran while one was open for 0% -> 2% of each run, Pallas kernels for 0% -> 0%
where the time goes in v5:
time: 147 us
  blocking collectives  106 us (72%)
  starting transfers between devices  15.9 us (11%)
  waiting for transfers between devices  13.3 us (9%)
  Pallas kernels  8.65 us (6%)
    all_to_all x1, blocking collectives, local(): lax.all_to_all(part.reshape(spots, TAIL, LANES), ('h', 'l'), 0, 0, tiled=...  48.5 us
    all_to_all x1, blocking collectives, local(): part = lax.all_to_all(part, ('y', 'x'), 0, 0, tiled=True)  27 us
    all_to_all x1, blocking collectives, local(): lax.all_to_all(part, ('x', 'l'), 0, 0, tiled=True)  16.6 us
    all_to_all x1, starting transfers between devices, local(): moved = lax.all_to_all(sent, ('x', 'l'), 0, 0, tiled=True)  15.9 us
    all_to_all x1, waiting for transfers between devices, local(): moved = lax.all_to_all(sent, ('x', 'l'), 0, 0, tiled=True)  13.3 us
    all_gather x1, blocking collectives, local(): wide = lax.all_gather(part, 'c', axis=0, tiled=True)  5.72 us
    pallas_call x1, Pallas kernels, local(): call(functools.partial(middle_kernel, dims), (shape((y_n * x_n, rows * ha...  5.37 us
    all_gather x1, blocking collectives, local(): pooled = lax.all_gather(pooled, 'c', axis=0, tiled=True)  4.11 us
  transfers between devices with their start and end apart: 1, of which 1 were waited for; matrix products, arithmetic and copies ran while one was open for 2% of the time, Pallas kernels for 0%

profile of v5, /device:TPU:1, one launch (start us, length us, event | category | flops | bytes accessed | tf_op | source)
XLA Modules:
  0.0 146.8 jit_solution(18243219381999192916)
XLA Ops:
  0.6 0.0 copy-start
  0.6 2.0 %shard_map.94 = bf16[32,4,1152]{2,1,0:T(4,128)(2,1)} custom-call(bf16[128,1024]{1,0:T(8,128)(2,1)} %bitcast.13, s32[1,128]{1,0:T(1,128)} %order_ref.3, f32[1,128]{1,0:T(1,128)} %cot_ref.1), custom_call_target="tpu_custom_call" | custom-call | tf_op jit(solution)/shard_map/pallas_call | solution.py:254
  2.6 15.9 %all-to-all-start = ((bf16[32,4,1152]{2,1,0:T(4,128)(2,1)}), bf16[32,4,1152]{2,1,0:T(4,128)(2,1)S(1)}, u32[]{:S(2)}, u32[]{:S(2)}) async-start(bf16[32,4,1152]{2,1,0:T(4,128)(2,1)} %shard_map.94), calls=%async_computation | async-start | bytes 589824 | tf_op jit(solution)/shard_map/all_to_all | solution.py:257
  18.6 0.7 broadcast_in_dim.15.bias_ref
  19.3 0.9 convert_reduce_fusion
  20.1 0.0 copy-done
  20.1 1.0 fusion
  21.1 4.1 %all_gather.10.pooled_ref = bf16[256,1536]{1,0:T(8,128)(2,1)S(1)} all-gather(bf16[128,1536]{1,0:T(8,128)(2,1)S(1)} %fusion), channel_id=1, replica_groups=mesh['y'=4,'h'=4,'x'=4,'l'=8,'c'=2] {'c'}, dimensions={0}, use_global_device_ids=true | all-gather | bytes 1179648 | tf_op jit(solution)/shard_map/all_gather | solution.py:265
  25.2 13.3 %all-to-all-done = bf16[32,4,1152]{2,1,0:T(4,128)(2,1)S(1)} async-done(((bf16[32,4,1152]{2,1,0:T(4,128)(2,1)}), bf16[32,4,1152]{2,1,0:T(4,128)(2,1)S(1)}, u32[]{:S(2)}, u32[]{:S(2)}) %all-to-all-start) | async-done | bytes 294944 | tf_op jit(solution)/shard_map/all_to_all | solution.py:257
  38.5 0.1 reshape.96
  38.6 3.7 %all_gather.9.both_ref = bf16[256,1152]{1,0:T(8,128)(2,1)S(1)} all-gather(bf16[128,1152]{1,0:T(8,128)(2,1)S(1)} %reshape.96), channel_id=1, replica_groups=mesh['y'=4,'h'=4,'x'=4,'l'=8,'c'=2] {'c'}, dimensions={0}, use_global_device_ids=true | all-gather | bytes 884736 | tf_op jit(solution)/shard_map/all_gather | solution.py:267
  42.3 5.4 %shard_map.95 = (bf16[16,400,128]{2,1,0:T(8,128)(2,1)S(1)}, f32[40,128]{1,0:T(8,128)S(1)}) custom-call(s32[1]{0:T(128)} %bitcast.core_ref, s32[1]{0:T(128)} %bitcast.1.high_ref, bf16[256,1152]{1,0:T(8,128)(2,1)S(1)} %all_gather.9.both_ref, bf16[256,1536]{1,0:T(8,128)(2,1)S(1)} %all_gather.10.pooled_ref, bf16[1024,1536]{1,0:T(8,128)(2,1)} %weight_ref.1, ...), custom_call_target="tpu_custom_call" | custom-call | tf_op jit(solution)/shard_map/pallas_call | solution.py:270
  47.7 27.0 %all_to_all.20.part_ref = bf16[16,400,128]{2,1,0:T(8,128)(2,1)S(1)} all-to-all(bf16[16,400,128]{2,1,0:T(8,128)(2,1)S(1)} %get-tuple-element.10), channel_id=1, replica_groups=mesh['y'=4,'h'=4,'x'=4,'l'=8,'c'=2] {'y','x'}, dimensions={0} | all-to-all | bytes 3276800 | tf_op jit(solution)/shard_map/all_to_all | solution.py:287
  74.7 0.0 copy-start.1
  74.7 0.3 shard_map.96
  75.0 48.5 %all_to_all.21.part_ref = bf16[32,16,128]{2,1,0:T(8,128)(2,1)S(1)} all-to-all(bf16[32,16,128]{2,1,0:T(8,128)(2,1)S(1)} %bitcast.12), channel_id=1, replica_groups=mesh['y'=4,'h'=4,'x'=4,'l'=8,'c'=2] {'h','l'}, dimensions={0} | all-to-all | bytes 262144 | tf_op jit(solution)/shard_map/all_to_all | solution.py:296
  123.5 0.1 shard_map.97
  123.5 16.6 %all_to_all.22 = bf16[32,16,128]{2,1,0:T(8,128)(2,1)S(1)} all-to-all(bf16[32,16,128]{2,1,0:T(8,128)(2,1)S(1)} %shard_map.97), channel_id=1, replica_groups=mesh['y'=4,'h'=4,'x'=4,'l'=8,'c'=2] {'x','l'}, dimensions={0} | all-to-all | bytes 262144 | tf_op jit(solution)/shard_map/all_to_all | solution.py:298
  140.1 5.7 %all_gather.11.both_ref = bf16[1024,128]{1,0:T(8,128)(2,1)S(1)} all-gather(bf16[512,128]{1,0:T(8,128)(2,1)S(1)} %bitcast.10), channel_id=1, replica_groups=mesh['y'=4,'h'=4,'x'=4,'l'=8,'c'=2] {'c'}, dimensions={0}, use_global_device_ids=true | all-gather | bytes 393216 | tf_op jit(solution)/shard_map/all_gather | solution.py:299
  145.8 0.0 copy-done.1
  145.8 1.0 shard_map.98
  (2 shorter events, 0.0 us)
Async XLA Ops:
  0.6 19.5 %copy-start = (bf16[1,256,1536]{2,1,0:T(8,128)(2,1)S(1)}, bf16[1,256,1536]{2,1,0:T(8,128)(2,1)}, u32[]{:S(2)}) copy-start(bf16[1,256,1536]{2,1,0:T(8,128)(2,1)} %param.10) | copy-start | bytes 2359300
  2.6 35.9 %all-to-all-start = ((bf16[32,4,1152]{2,1,0:T(4,128)(2,1)}), bf16[32,4,1152]{2,1,0:T(4,128)(2,1)S(1)}, u32[]{:S(2)}, u32[]{:S(2)}) async-start(bf16[32,4,1152]{2,1,0:T(4,128)(2,1)} %shard_map.94), calls=%async_computation | async-start | bytes 589824 | tf_op jit(solution)/shard_map/all_to_all | solution.py:257
  74.7 71.1 %copy-start.1 = (s32[1,128]{1,0:T(1,128)S(1)}, s32[1,128]{1,0:T(1,128)}, u32[]{:S(2)}) copy-start(s32[1,128]{1,0:T(1,128)} %order_ref.3) | copy-start | bytes 1540

commit v6 on v3

--- a/solution.py
+++ b/solution.py
@@ -26,7 +26,7 @@
     return head, (values - head.astype(F32)).astype(BF)
 
 
-def call(body, outs, ins, scratch=(), limit=40):
+def call(body, outs, ins, scratch=(), limit=16):
     return pl.pallas_call(
         body,
         out_shape=outs,
@@ -56,10 +56,8 @@
         out_ref[p] = jnp.concatenate([rows[at], cols[at]], axis=1).astype(BF)
 
 
-def pool_kernel(dims, patch_ref, slot_ref, weight_ref, pooled_ref, near_ref, sem):
+def pool_kernel(dims, patch_ref, slot_ref, pooled_ref):
     y_n, h_n, x_n, l_n, c_n, two = dims
-    fetch = pltpu.make_async_copy(weight_ref, near_ref, sem)
-    fetch.start()
     tokens, patches = pooled_ref.shape[0], patch_ref.shape[0]
     shape = (tokens, patches)
     row = iota(shape, 0)
@@ -70,15 +68,20 @@
     counts = jnp.sum(match, axis=1, keepdims=True)
     totals = jnp.dot(match.astype(BF), patch_ref[...], preferred_element_type=F32)
     pooled_ref[...] = (totals / counts).astype(BF)
-    fetch.wait()
 
 
 def middle_kernel(
-    dims, core_ref, high_ref, both_ref, pooled_ref, weight_ref, bias_ref, part_ref, back_ref, proj, target, grads
+    dims, core_ref, high_ref, both_ref, pooled_ref, weight_ref, bias_ref, part_ref, back_ref,
+    proj, target, grads, rows_held, acts, pooled, sem
 ):
     y_n, h_n, x_n, l_n, c_n, two = dims
     near, per = x_n * l_n, c_n * two
-    tokens, units = both_ref.shape[0], both_ref.shape[1] - LANES
+    tokens, units = acts.shape
+    fetch = pltpu.make_async_copy(pooled_ref, pooled, sem)
+    fetch.start()
+    for p in range(both_ref.shape[0]):
+        rows_held[p * per : (p + 1) * per, :] = both_ref[p].astype(F32)
+    acts[...] = rows_held[:, :units].astype(BF)
     width = weight_ref.shape[1]
     half = width // c_n
     single = tokens // c_n
@@ -88,24 +91,26 @@
         (row // two) % c_n * single + row // single * (near * two) + row // per % near * two + row % two
     )
     turn = jnp.where(wanted == iota((tokens, tokens), 1), 1.0, 0.0).astype(BF)
-    acts = both_ref[:, :units]
     step = 256
     s_pp = jnp.zeros((tokens, 1), F32)
     s_tt = jnp.zeros((tokens, 1), F32)
     s_pt = jnp.zeros((tokens, 1), F32)
     for at in range(0, width, step):
         cut = slice(at, at + step)
-        p = jnp.dot(acts, weight_ref[:, cut], preferred_element_type=F32) + bias_ref[:, cut]
-        t = jnp.dot(turn, pooled_ref[:, cut], preferred_element_type=F32)
+        p = jnp.dot(acts[...], weight_ref[:, cut], preferred_element_type=F32) + bias_ref[:, cut]
         proj[:, cut] = p
+        s_pp = s_pp + jnp.sum(p * p, axis=1, keepdims=True)
+    fetch.wait()
+    for at in range(0, width, step):
+        cut = slice(at, at + step)
+        t = jnp.dot(turn, pooled[:, cut], preferred_element_type=F32)
         target[:, cut] = t
-        s_pp = s_pp + jnp.sum(p * p, axis=1, keepdims=True)
         s_tt = s_tt + jnp.sum(t * t, axis=1, keepdims=True)
-        s_pt = s_pt + jnp.sum(p * t, axis=1, keepdims=True)
+        s_pt = s_pt + jnp.sum(proj[:, cut] * t, axis=1, keepdims=True)
     inv_proj = lax.rsqrt(s_pp + 1e-06)
     inv_target = lax.rsqrt(s_tt + 1e-06)
     cosine = s_pt * inv_proj * inv_target
-    terms = both_ref[:, units:].astype(F32)
+    terms = rows_held[:, units:]
     cot = (terms[:, 2:3] + terms[:, 1:2]) + terms[:, 0:1]
     scale_t = inv_proj * inv_target
     scale_p = cosine * inv_proj * inv_proj
@@ -263,15 +268,13 @@
         hidden[0], order, cotangent
     )
     moved = lax.all_to_all(sent, ("x", "l"), 0, 0, tiled=True)
-    pooled, weight = call(
-        functools.partial(pool_kernel, dims),
-        (shape((tokens, width), BF), shape(weight.shape, BF)),
-        [VMEM, VMEM, pl.BlockSpec(memory_space=pl.ANY)],
-        [pltpu.SemaphoreType.DMA],
-    )(patches, slots, weight)
+    pooled = call(
+        functools.partial(pool_kernel, dims), shape((tokens, width), BF), [VMEM] * 2, limit=60
+    )(patches, slots)
     pooled = lax.all_gather(pooled, "c", axis=0, tiled=True)
-
-    both = lax.all_gather(moved.reshape(tokens, units + LANES), "c", axis=0, tiled=True)
+    pooled = pltpu.with_memory_space_constraint(pooled, pltpu.HBM)
+
+    both = lax.all_gather(moved, "c", axis=0, tiled=True)
     rows = units // (y_n * x_n)
     lines = half // LANES * LINE_ROWS
     part, back = call(
@@ -280,11 +283,15 @@
             shape((y_n * x_n, rows * half // LANES + TAIL, LANES), BF),
             shape((near + 8, LANES), F32),
         ),
-        [SMEM] * 2 + [VMEM] * 4,
+        [SMEM] * 2 + [VMEM, pl.BlockSpec(memory_space=pltpu.HBM), VMEM, VMEM],
         [
             pltpu.VMEM((c_n * tokens, width), F32),
             pltpu.VMEM((c_n * tokens, width), F32),
             pltpu.VMEM((c_n, c_n * tokens, half), BF),
+            pltpu.VMEM((c_n * tokens, units + LANES), F32),
+            pltpu.VMEM((c_n * tokens, units), BF),
+            pltpu.VMEM((c_n * tokens, width), BF),
+            pltpu.SemaphoreType.DMA,
         ],
     )(core, high, both, pooled, weight, bias[None, :])
 

time: 147 us -> 145 us (0.986)
  local copies, waits for them, and re-layouts: 6.58 us -> 0.86 us
  Pallas kernels: 6.23 us -> 9.24 us
    unnamed x10 -> x4, local copies, waits for them, and re-layouts: 4.84 us -> 0.01 us
    pallas_call x1, Pallas kernels: 0.49 us -> 2.25 us  [local(): call(functools.partial(pool_kernel, dims), shape((tokens, width), BF), [V...]
  transfers between devices with their start and end apart: 1 -> 1, of which waited for: 1 -> 1; matrix products, arithmetic and copies ran while one was open for 0% -> 1% of each run, Pallas kernels for 0% -> 2%
where the time goes in v6:
time: 145 us
  blocking collectives  107 us (74%)
  starting transfers between devices  15.9 us (11%)
  waiting for transfers between devices  10.9 us (8%)
  Pallas kernels  9.24 us (6%)
    all_to_all x1, blocking collectives, local(): lax.all_to_all(part.reshape(spots, TAIL, LANES), ('h', 'l'), 0, 0, tiled=...  48.5 us
    all_to_all x1, blocking collectives, local(): part = lax.all_to_all(part, ('y', 'x'), 0, 0, tiled=True)  27 us
    all_to_all x1, blocking collectives, local(): lax.all_to_all(part, ('x', 'l'), 0, 0, tiled=True)  16.6 us
    all_to_all x1, starting transfers between devices, local(): moved = lax.all_to_all(sent, ('x', 'l'), 0, 0, tiled=True)  15.9 us
    all_to_all x1, waiting for transfers between devices, local(): moved = lax.all_to_all(sent, ('x', 'l'), 0, 0, tiled=True)  10.9 us
    all_gather x1, blocking collectives, local(): pooled = lax.all_gather(pooled, 'c', axis=0, tiled=True)  6 us
    all_gather x1, blocking collectives, local(): wide = lax.all_gather(part, 'c', axis=0, tiled=True)  5.73 us
    pallas_call x1, Pallas kernels, local(): call(functools.partial(middle_kernel, dims), (shape((y_n * x_n, rows * ha...  3.8 us
  transfers between devices with their start and end apart: 1, of which 1 were waited for; matrix products, arithmetic and copies ran while one was open for 1% of the time, Pallas kernels for 2%

profile of v6, /device:TPU:1, one launch (start us, length us, event | category | flops | bytes accessed | tf_op | source)
XLA Modules:
  0.0 145.1 jit_solution(15723078796231566249)
XLA Ops:
  0.6 1.9 %shard_map.94 = bf16[32,4,1152]{2,1,0:T(4,128)(2,1)} custom-call(bf16[128,1024]{1,0:T(8,128)(2,1)} %bitcast.11, s32[1,128]{1,0:T(1,128)} %order_ref.3, f32[1,128]{1,0:T(1,128)} %cot_ref.1), custom_call_target="tpu_custom_call" | custom-call | tf_op jit(solution)/shard_map/pallas_call | solution.py:267
  2.5 15.9 %all-to-all-start = ((bf16[32,4,1152]{2,1,0:T(4,128)(2,1)}), bf16[32,4,1152]{2,1,0:T(4,128)(2,1)S(1)}, u32[]{:S(2)}, u32[]{:S(2)}) async-start(bf16[32,4,1152]{2,1,0:T(4,128)(2,1)} %shard_map.94), calls=%async_computation | async-start | bytes 589824 | tf_op jit(solution)/shard_map/all_to_all | solution.py:270
  18.4 0.0 copy-start
  18.5 0.9 broadcast_in_dim.11.bias_ref
  19.3 2.2 %shard_map.95 = bf16[128,1536]{1,0:T(8,128)(2,1)} custom-call(bf16[256,1536]{1,0:T(8,128)(2,1)} %bitcast.10, s32[1,256]{1,0:T(1,128)} %slot_ref.1), custom_call_target="tpu_custom_call" | custom-call | tf_op jit(solution)/shard_map/pallas_call | solution.py:271
  21.6 6.0 %all_gather.10.pooled_ref = bf16[256,1536]{1,0:T(8,128)(2,1)} all-gather(bf16[128,1536]{1,0:T(8,128)(2,1)} %shard_map.95), channel_id=1, replica_groups=mesh['y'=4,'h'=4,'x'=4,'l'=8,'c'=2] {'c'}, dimensions={0}, use_global_device_ids=true | all-gather | bytes 1179648 | tf_op jit(solution)/shard_map/all_gather | solution.py:274
  27.6 10.9 %all-to-all-done = bf16[32,4,1152]{2,1,0:T(4,128)(2,1)S(1)} async-done(((bf16[32,4,1152]{2,1,0:T(4,128)(2,1)}), bf16[32,4,1152]{2,1,0:T(4,128)(2,1)S(1)}, u32[]{:S(2)}, u32[]{:S(2)}) %all-to-all-start) | async-done | bytes 294944 | tf_op jit(solution)/shard_map/all_to_all | solution.py:270
  38.5 3.7 %all_gather.9.both_ref = bf16[64,4,1152]{2,1,0:T(4,128)(2,1)S(1)} all-gather(bf16[32,4,1152]{2,1,0:T(4,128)(2,1)S(1)} %all-to-all-done), channel_id=1, replica_groups=mesh['y'=4,'h'=4,'x'=4,'l'=8,'c'=2] {'c'}, dimensions={0}, use_global_device_ids=true | all-gather | bytes 884736 | tf_op jit(solution)/shard_map/all_gather | solution.py:277
  42.1 0.0 copy-done
  42.2 3.8 %shard_map.96 = (bf16[16,400,128]{2,1,0:T(8,128)(2,1)S(1)}, f32[40,128]{1,0:T(8,128)S(1)}) custom-call(s32[1]{0:T(128)} %bitcast.core_ref, s32[1]{0:T(128)} %bitcast.1.high_ref, bf16[64,4,1152]{2,1,0:T(4,128)(2,1)S(1)} %all_gather.9.both_ref, bf16[256,1536]{1,0:T(8,128)(2,1)} %all_gather.10.pooled_ref, bf16[1024,1536]{1,0:T(8,128)(2,1)S(1)} %copy-done, ...), custom_call_target="tpu_custom_call" | custom-call | tf_op jit(solution)/shard_map/pallas_call | solution.py:280
  46.0 27.0 %all_to_all.20.part_ref = bf16[16,400,128]{2,1,0:T(8,128)(2,1)S(1)} all-to-all(bf16[16,400,128]{2,1,0:T(8,128)(2,1)S(1)} %get-tuple-element.10), channel_id=1, replica_groups=mesh['y'=4,'h'=4,'x'=4,'l'=8,'c'=2] {'y','x'}, dimensions={0} | all-to-all | bytes 3276800 | tf_op jit(solution)/shard_map/all_to_all | solution.py:298
  72.9 0.0 copy-start.1
  72.9 0.3 shard_map.97
  73.2 48.5 %all_to_all.21.part_ref = bf16[32,16,128]{2,1,0:T(8,128)(2,1)S(1)} all-to-all(bf16[32,16,128]{2,1,0:T(8,128)(2,1)S(1)} %bitcast.9), channel_id=1, replica_groups=mesh['y'=4,'h'=4,'x'=4,'l'=8,'c'=2] {'h','l'}, dimensions={0} | all-to-all | bytes 262144 | tf_op jit(solution)/shard_map/all_to_all | solution.py:307
  121.7 0.1 shard_map.98
  121.7 16.6 %all_to_all.22 = bf16[32,16,128]{2,1,0:T(8,128)(2,1)S(1)} all-to-all(bf16[32,16,128]{2,1,0:T(8,128)(2,1)S(1)} %shard_map.98), channel_id=1, replica_groups=mesh['y'=4,'h'=4,'x'=4,'l'=8,'c'=2] {'x','l'}, dimensions={0} | all-to-all | bytes 262144 | tf_op jit(solution)/shard_map/all_to_all | solution.py:309
  138.3 5.7 %all_gather.11.both_ref = bf16[1024,128]{1,0:T(8,128)(2,1)S(1)} all-gather(bf16[512,128]{1,0:T(8,128)(2,1)S(1)} %bitcast.7), channel_id=1, replica_groups=mesh['y'=4,'h'=4,'x'=4,'l'=8,'c'=2] {'c'}, dimensions={0}, use_global_device_ids=true | all-gather | bytes 393216 | tf_op jit(solution)/shard_map/all_gather | solution.py:310
  144.1 0.0 copy-done.1
  144.1 1.0 shard_map.99
Async XLA Ops:
  2.5 35.9 %all-to-all-start = ((bf16[32,4,1152]{2,1,0:T(4,128)(2,1)}), bf16[32,4,1152]{2,1,0:T(4,128)(2,1)S(1)}, u32[]{:S(2)}, u32[]{:S(2)}) async-start(bf16[32,4,1152]{2,1,0:T(4,128)(2,1)} %shard_map.94), calls=%async_computation | async-start | bytes 589824 | tf_op jit(solution)/shard_map/all_to_all | solution.py:270
  18.4 23.7 %copy-start = (bf16[1024,1536]{1,0:T(8,128)(2,1)S(1)}, bf16[1024,1536]{1,0:T(8,128)(2,1)}, u32[]{:S(2)}) copy-start(bf16[1024,1536]{1,0:T(8,128)(2,1)} %weight_ref.1) | copy-start | bytes 9437188
  72.9 71.1 %copy-start.1 = (s32[1,128]{1,0:T(1,128)S(1)}, s32[1,128]{1,0:T(1,128)}, u32[]{:S(2)}) copy-start(s32[1,128]{1,0:T(1,128)} %order_ref.3) | copy-start | bytes 1540

commit v7 on v6

--- a/solution.py
+++ b/solution.py
@@ -72,16 +72,19 @@
 
 def middle_kernel(
     dims, core_ref, high_ref, both_ref, pooled_ref, weight_ref, bias_ref, part_ref, back_ref,
-    proj, target, grads, rows_held, acts, pooled, sem
+    proj, target, grads, terms, acts, pooled, sem
 ):
     y_n, h_n, x_n, l_n, c_n, two = dims
     near, per = x_n * l_n, c_n * two
     tokens, units = acts.shape
     fetch = pltpu.make_async_copy(pooled_ref, pooled, sem)
     fetch.start()
-    for p in range(both_ref.shape[0]):
-        rows_held[p * per : (p + 1) * per, :] = both_ref[p].astype(F32)
-    acts[...] = rows_held[:, :units].astype(BF)
+    join = TAIL // per
+    for g in range(tokens // TAIL):
+        tall = jnp.concatenate([both_ref[g * join + i].astype(F32) for i in range(join)], axis=0)
+        at = slice(g * TAIL, (g + 1) * TAIL)
+        acts[at, :] = tall[:, :units].astype(BF)
+        terms[at, :] = tall[:, units:]
     width = weight_ref.shape[1]
     half = width // c_n
     single = tokens // c_n
@@ -110,7 +113,6 @@
     inv_proj = lax.rsqrt(s_pp + 1e-06)
     inv_target = lax.rsqrt(s_tt + 1e-06)
     cosine = s_pt * inv_proj * inv_target
-    terms = rows_held[:, units:]
     cot = (terms[:, 2:3] + terms[:, 1:2]) + terms[:, 0:1]
     scale_t = inv_proj * inv_target
     scale_p = cosine * inv_proj * inv_proj
@@ -127,11 +129,11 @@
         tail = jnp.where(tail_row == 0, high, jnp.where(tail_row == 1, total - high, 0.0)).astype(BF)
         for k in range(step // LANES):
             block = at // LANES + k
-            piece = block // y_blocks * x_n + block % y_blocks
+            piece = block % y_blocks * y_n + block // y_blocks
             part_ref[piece, main:, :] = tail[:, k * LANES : (k + 1) * LANES]
     for y in range(y_n):
         for x in range(y_blocks, x_n):
-            part_ref[y * x_n + x, main:, :] = jnp.zeros((TAIL, LANES), BF)
+            part_ref[x * y_n + y, main:, :] = jnp.zeros((TAIL, LANES), BF)
     lane = iota((tokens, LANES), 1)
     high, low = split_two(cosine)
     spot = iota((tokens, LANES), 0) % per == lane
@@ -156,7 +158,7 @@
                 start = (h * x_n + x) * chunk
                 for k in range(half // LANES):
                     to = (k * h_n + h) * chunk
-                    part_ref[y * x_n + x, to : to + chunk, :] = product[
+                    part_ref[x * y_n + y, to : to + chunk, :] = product[
                         start : start + chunk, k * LANES : (k + 1) * LANES
                     ]
 
@@ -182,7 +184,7 @@
         for h in range(h_n):
             for r in range(LINE_ROWS):
                 at = (h * LINE_ROWS + r) * l_n
-                spread[pl.ds(h * l_n * group + k * LINE_ROWS + r, l_n, stride=group), :] = total[at : at + l_n]
+                spread[pl.ds(h * group + k * LINE_ROWS + r, l_n, stride=h_n * group), :] = total[at : at + l_n]
     tail = summed(main, TAIL)
     bias = tail[0:1] + tail[1:2]
     high = bias.astype(BF).astype(F32)
@@ -288,14 +290,14 @@
             pltpu.VMEM((c_n * tokens, width), F32),
             pltpu.VMEM((c_n * tokens, width), F32),
             pltpu.VMEM((c_n, c_n * tokens, half), BF),
-            pltpu.VMEM((c_n * tokens, units + LANES), F32),
+            pltpu.VMEM((c_n * tokens, LANES), F32),
             pltpu.VMEM((c_n * tokens, units), BF),
             pltpu.VMEM((c_n * tokens, width), BF),
             pltpu.SemaphoreType.DMA,
         ],
     )(core, high, both, pooled, weight, bias[None, :])
 
-    part = lax.all_to_all(part, ("y", "x"), 0, 0, tiled=True)
+    part = lax.all_to_all(part, ("x", "y"), 0, 0, tiled=True)
     spots = h_n * l_n
     part = call(
         functools.partial(plane_kernel, dims),
@@ -304,7 +306,7 @@
         [pltpu.VMEM((spots * TAIL, LANES), F32)],
     )(part)
     part, back = lax.optimization_barrier((part, back))
-    part = lax.all_to_all(part.reshape(spots, TAIL, LANES), ("h", "l"), 0, 0, tiled=True)
+    part = lax.all_to_all(part.reshape(spots, TAIL, LANES), ("l", "h"), 0, 0, tiled=True)
     part = call(functools.partial(line_kernel, lines), shape((near, TAIL, LANES), BF), [VMEM] * 2)(part, back)
     part = lax.all_to_all(part, ("x", "l"), 0, 0, tiled=True).reshape(near * TAIL, LANES)
     wide = lax.all_gather(part, "c", axis=0, tiled=True)

time: 145 us -> 145 us (level)
    all_to_all x2, blocking collectives: 75.5 us -> 69.8 us  [the longest x1 42.8 us: local(): lax.all_to_all(part.reshape(spots, TAIL, LANES), ('l', 'h'), 0, 0, tiled=...]
    all_to_all x1, blocking collectives: 16.6 us -> 21.8 us  [local(): lax.all_to_all(part, ('x', 'l'), 0, 0, tiled=True)]
where the time goes in v7:
time: 145 us
  blocking collectives  107 us (74%)
  starting transfers between devices  15.9 us (11%)
  waiting for transfers between devices  10.9 us (8%)
  Pallas kernels  9.25 us (6%)
    all_to_all x1, blocking collectives, local(): lax.all_to_all(part.reshape(spots, TAIL, LANES), ('l', 'h'), 0, 0, tiled=...  42.8 us
    all_to_all x1, blocking collectives, local(): part = lax.all_to_all(part, ('x', 'y'), 0, 0, tiled=True)  27.1 us
    all_to_all x1, blocking collectives, local(): lax.all_to_all(part, ('x', 'l'), 0, 0, tiled=True)  21.8 us
    all_to_all x1, starting transfers between devices, local(): moved = lax.all_to_all(sent, ('x', 'l'), 0, 0, tiled=True)  15.9 us
    all_to_all x1, waiting for transfers between devices, local(): moved = lax.all_to_all(sent, ('x', 'l'), 0, 0, tiled=True)  10.9 us
    all_gather x1, blocking collectives, local(): pooled = lax.all_gather(pooled, 'c', axis=0, tiled=True)  6 us
    all_gather x1, blocking collectives, local(): wide = lax.all_gather(part, 'c', axis=0, tiled=True)  5.9 us
    pallas_call x1, Pallas kernels, local(): call(functools.partial(middle_kernel, dims), (shape((y_n * x_n, rows * ha...  3.78 us
  transfers between devices with their start and end apart: 1, of which 1 were waited for; matrix products, arithmetic and copies ran while one was open for 1% of the time, Pallas kernels for 2%

profile of v7, /device:TPU:1, one launch (start us, length us, event | category | flops | bytes accessed | tf_op | source)
XLA Modules:
  0.0 144.9 jit_solution(3671042767048315463)
XLA Ops:
  0.6 1.9 %shard_map.94 = bf16[32,4,1152]{2,1,0:T(4,128)(2,1)} custom-call(bf16[128,1024]{1,0:T(8,128)(2,1)} %bitcast.11, s32[1,128]{1,0:T(1,128)} %order_ref.3, f32[1,128]{1,0:T(1,128)} %cot_ref.1), custom_call_target="tpu_custom_call" | custom-call | tf_op jit(solution)/shard_map/pallas_call | solution.py:269
  2.5 15.9 %all-to-all-start = ((bf16[32,4,1152]{2,1,0:T(4,128)(2,1)}), bf16[32,4,1152]{2,1,0:T(4,128)(2,1)S(1)}, u32[]{:S(2)}, u32[]{:S(2)}) async-start(bf16[32,4,1152]{2,1,0:T(4,128)(2,1)} %shard_map.94), calls=%async_computation | async-start | bytes 589824 | tf_op jit(solution)/shard_map/all_to_all | solution.py:272
  18.4 0.0 copy-start
  18.5 0.9 broadcast_in_dim.11.bias_ref
  19.3 2.2 %shard_map.95 = bf16[128,1536]{1,0:T(8,128)(2,1)} custom-call(bf16[256,1536]{1,0:T(8,128)(2,1)} %bitcast.10, s32[1,256]{1,0:T(1,128)} %slot_ref.1), custom_call_target="tpu_custom_call" | custom-call | tf_op jit(solution)/shard_map/pallas_call | solution.py:273
  21.6 6.0 %all_gather.10.pooled_ref = bf16[256,1536]{1,0:T(8,128)(2,1)} all-gather(bf16[128,1536]{1,0:T(8,128)(2,1)} %shard_map.95), channel_id=1, replica_groups=mesh['y'=4,'h'=4,'x'=4,'l'=8,'c'=2] {'c'}, dimensions={0}, use_global_device_ids=true | all-gather | bytes 1179648 | tf_op jit(solution)/shard_map/all_gather | solution.py:276
  27.6 10.9 %all-to-all-done = bf16[32,4,1152]{2,1,0:T(4,128)(2,1)S(1)} async-done(((bf16[32,4,1152]{2,1,0:T(4,128)(2,1)}), bf16[32,4,1152]{2,1,0:T(4,128)(2,1)S(1)}, u32[]{:S(2)}, u32[]{:S(2)}) %all-to-all-start) | async-done | bytes 294944 | tf_op jit(solution)/shard_map/all_to_all | solution.py:272
  38.5 3.7 %all_gather.9.both_ref = bf16[64,4,1152]{2,1,0:T(4,128)(2,1)S(1)} all-gather(bf16[32,4,1152]{2,1,0:T(4,128)(2,1)S(1)} %all-to-all-done), channel_id=1, replica_groups=mesh['y'=4,'h'=4,'x'=4,'l'=8,'c'=2] {'c'}, dimensions={0}, use_global_device_ids=true | all-gather | bytes 884736 | tf_op jit(solution)/shard_map/all_gather | solution.py:279
  42.1 0.0 copy-done
  42.2 3.8 %shard_map.96 = (bf16[16,400,128]{2,1,0:T(8,128)(2,1)S(1)}, f32[40,128]{1,0:T(8,128)S(1)}) custom-call(s32[1]{0:T(128)} %bitcast.core_ref, s32[1]{0:T(128)} %bitcast.1.high_ref, bf16[64,4,1152]{2,1,0:T(4,128)(2,1)S(1)} %all_gather.9.both_ref, bf16[256,1536]{1,0:T(8,128)(2,1)} %all_gather.10.pooled_ref, bf16[1024,1536]{1,0:T(8,128)(2,1)S(1)} %copy-done, ...), custom_call_target="tpu_custom_call" | custom-call | tf_op jit(solution)/shard_map/pallas_call | solution.py:282
  45.9 27.1 %all_to_all.20.part_ref = bf16[16,400,128]{2,1,0:T(8,128)(2,1)S(1)} all-to-all(bf16[16,400,128]{2,1,0:T(8,128)(2,1)S(1)} %get-tuple-element.10), channel_id=1, replica_groups=mesh['y'=4,'h'=4,'x'=4,'l'=8,'c'=2] {'x','y'}, dimensions={0} | all-to-all | bytes 3276800 | tf_op jit(solution)/shard_map/all_to_all | solution.py:300
  73.0 0.0 copy-start.1
  73.0 0.3 shard_map.97
  73.3 42.8 %all_to_all.21.part_ref = bf16[32,16,128]{2,1,0:T(8,128)(2,1)S(1)} all-to-all(bf16[32,16,128]{2,1,0:T(8,128)(2,1)S(1)} %bitcast.9), channel_id=1, replica_groups=mesh['y'=4,'h'=4,'x'=4,'l'=8,'c'=2] {'l','h'}, dimensions={0} | all-to-all | bytes 262144 | tf_op jit(solution)/shard_map/all_to_all | solution.py:309
  116.1 0.1 shard_map.98
  116.2 21.8 %all_to_all.22 = bf16[32,16,128]{2,1,0:T(8,128)(2,1)S(1)} all-to-all(bf16[32,16,128]{2,1,0:T(8,128)(2,1)S(1)} %shard_map.98), channel_id=1, replica_groups=mesh['y'=4,'h'=4,'x'=4,'l'=8,'c'=2] {'x','l'}, dimensions={0} | all-to-all | bytes 262144 | tf_op jit(solution)/shard_map/all_to_all | solution.py:311
  138.0 5.9 %all_gather.11.both_ref = bf16[1024,128]{1,0:T(8,128)(2,1)S(1)} all-gather(bf16[512,128]{1,0:T(8,128)(2,1)S(1)} %bitcast.7), channel_id=1, replica_groups=mesh['y'=4,'h'=4,'x'=4,'l'=8,'c'=2] {'c'}, dimensions={0}, use_global_device_ids=true | all-gather | bytes 393216 | tf_op jit(solution)/shard_map/all_gather | solution.py:312
  143.9 0.0 copy-done.1
  143.9 1.0 shard_map.99
Async XLA Ops:
  2.5 35.9 %all-to-all-start = ((bf16[32,4,1152]{2,1,0:T(4,128)(2,1)}), bf16[32,4,1152]{2,1,0:T(4,128)(2,1)S(1)}, u32[]{:S(2)}, u32[]{:S(2)}) async-start(bf16[32,4,1152]{2,1,0:T(4,128)(2,1)} %shard_map.94), calls=%async_computation | async-start | bytes 589824 | tf_op jit(solution)/shard_map/all_to_all | solution.py:272
  18.4 23.7 %copy-start = (bf16[1024,1536]{1,0:T(8,128)(2,1)S(1)}, bf16[1024,1536]{1,0:T(8,128)(2,1)}, u32[]{:S(2)}) copy-start(bf16[1024,1536]{1,0:T(8,128)(2,1)} %weight_ref.1) | copy-start | bytes 9437188
  73.0 70.9 %copy-start.1 = (s32[1,128]{1,0:T(1,128)S(1)}, s32[1,128]{1,0:T(1,128)}, u32[]{:S(2)}) copy-start(s32[1,128]{1,0:T(1,128)} %order_ref.3) | copy-start | bytes 1540

commit v8 on v7

--- a/solution.py
+++ b/solution.py
@@ -15,6 +15,7 @@
 LINE_ROWS = 2
 VMEM = pl.BlockSpec(memory_space=pltpu.VMEM)
 SMEM = pl.BlockSpec(memory_space=pltpu.SMEM)
+HBM = pl.BlockSpec(memory_space=pltpu.HBM)
 
 
 def iota(shape, axis):
@@ -71,21 +72,19 @@
 
 
 def middle_kernel(
-    dims, core_ref, high_ref, both_ref, pooled_ref, weight_ref, bias_ref, part_ref, back_ref,
-    proj, target, grads, terms, acts, pooled, sem
+    dims, core_ref, high_ref, both_ref, pooled_ref, weight_ref, rest_ref, bias_ref, part_ref, back_ref,
+    proj, target, grads, held, pooled, sems
 ):
     y_n, h_n, x_n, l_n, c_n, two = dims
     near, per = x_n * l_n, c_n * two
-    tokens, units = acts.shape
-    fetch = pltpu.make_async_copy(pooled_ref, pooled, sem)
+    tokens, units = both_ref.shape[0], both_ref.shape[1] - LANES
+    first = weight_ref.shape[1]
+    fetch_rest = pltpu.make_async_copy(rest_ref.at[:, pl.ds(first, LANES)], held, sems.at[1])
+    fetch_rest.start()
+    fetch = pltpu.make_async_copy(pooled_ref, pooled, sems.at[0])
     fetch.start()
-    join = TAIL // per
-    for g in range(tokens // TAIL):
-        tall = jnp.concatenate([both_ref[g * join + i].astype(F32) for i in range(join)], axis=0)
-        at = slice(g * TAIL, (g + 1) * TAIL)
-        acts[at, :] = tall[:, :units].astype(BF)
-        terms[at, :] = tall[:, units:]
-    width = weight_ref.shape[1]
+    acts = both_ref[:, :units]
+    width = rest_ref.shape[1]
     half = width // c_n
     single = tokens // c_n
     core = core_ref[0]
@@ -98,9 +97,14 @@
     s_pp = jnp.zeros((tokens, 1), F32)
     s_tt = jnp.zeros((tokens, 1), F32)
     s_pt = jnp.zeros((tokens, 1), F32)
-    for at in range(0, width, step):
-        cut = slice(at, at + step)
-        p = jnp.dot(acts[...], weight_ref[:, cut], preferred_element_type=F32) + bias_ref[:, cut]
+    starts = list(range(0, first - step + 1, step))
+    blocks = [(at, step) for at in starts] + [(at, LANES) for at in range(len(starts) * step, width, LANES)]
+    for at, size in blocks:
+        cut = slice(at, at + size)
+        if at == first:
+            fetch_rest.wait()
+        block = held[...] if at == first else weight_ref[:, cut]
+        p = jnp.dot(acts, block, preferred_element_type=F32) + bias_ref[:, cut]
         proj[:, cut] = p
         s_pp = s_pp + jnp.sum(p * p, axis=1, keepdims=True)
     fetch.wait()
@@ -113,6 +117,7 @@
     inv_proj = lax.rsqrt(s_pp + 1e-06)
     inv_target = lax.rsqrt(s_tt + 1e-06)
     cosine = s_pt * inv_proj * inv_target
+    terms = both_ref[:, units:].astype(F32)
     cot = (terms[:, 2:3] + terms[:, 1:2]) + terms[:, 0:1]
     scale_t = inv_proj * inv_target
     scale_p = cosine * inv_proj * inv_proj
@@ -276,7 +281,7 @@
     pooled = lax.all_gather(pooled, "c", axis=0, tiled=True)
     pooled = pltpu.with_memory_space_constraint(pooled, pltpu.HBM)
 
-    both = lax.all_gather(moved, "c", axis=0, tiled=True)
+    both = lax.all_gather(moved.reshape(tokens, units + LANES), "c", axis=0, tiled=True)
     rows = units // (y_n * x_n)
     lines = half // LANES * LINE_ROWS
     part, back = call(
@@ -285,17 +290,16 @@
             shape((y_n * x_n, rows * half // LANES + TAIL, LANES), BF),
             shape((near + 8, LANES), F32),
         ),
-        [SMEM] * 2 + [VMEM, pl.BlockSpec(memory_space=pltpu.HBM), VMEM, VMEM],
+        [SMEM] * 2 + [VMEM, HBM, VMEM, HBM, VMEM],
         [
             pltpu.VMEM((c_n * tokens, width), F32),
             pltpu.VMEM((c_n * tokens, width), F32),
             pltpu.VMEM((c_n, c_n * tokens, half), BF),
-            pltpu.VMEM((c_n * tokens, LANES), F32),
-            pltpu.VMEM((c_n * tokens, units), BF),
+            pltpu.VMEM((units, LANES), BF),
             pltpu.VMEM((c_n * tokens, width), BF),
-            pltpu.SemaphoreType.DMA,
+            pltpu.SemaphoreType.DMA((2,)),
         ],
-    )(core, high, both, pooled, weight, bias[None, :])
+    )(core, high, both, pooled, weight[:, : width - LANES], pltpu.with_memory_space_constraint(weight, pltpu.HBM), bias[None, :])
 
     part = lax.all_to_all(part, ("x", "y"), 0, 0, tiled=True)
     spots = h_n * l_n

time: 145 us -> 145 us (level)
  local copies, waits for them, and re-layouts: 0.86 us -> 2.81 us
  waiting for transfers between devices: 10.9 us -> 9.1 us
    slice x0 -> x1, local copies, waits for them, and re-layouts: none -> 2.03 us  [local(): weight[:, :width - LANES]]
    all_to_all x1, waiting for transfers between devices: 10.9 us -> 9.1 us  [local(): moved = lax.all_to_all(sent, ('x', 'l'), 0, 0, tiled=True)]
  transfers between devices with their start and end apart: 1 -> 1, of which waited for: 1 -> 1; matrix products, arithmetic and copies ran while one was open for 1% -> 2% of each run, Pallas kernels for 2% -> 1%
where the time goes in v8:
time: 145 us; the launch traced here: 144 us
  blocking collectives  107 us (74%)
  starting transfers between devices  15.9 us (11%)
  waiting for transfers between devices  9.1 us (6%)
  Pallas kernels  8.57 us (6%)
  local copies, waits for them, and re-layouts  2.81 us (2%)
    all_to_all x1, blocking collectives, local(): lax.all_to_all(part.reshape(spots, TAIL, LANES), ('l', 'h'), 0, 0, tiled=...  42.8 us
    all_to_all x1, blocking collectives, local(): part = lax.all_to_all(part, ('x', 'y'), 0, 0, tiled=True)  27.1 us
    all_to_all x1, blocking collectives, local(): lax.all_to_all(part, ('x', 'l'), 0, 0, tiled=True)  21.8 us
    all_to_all x1, starting transfers between devices, local(): moved = lax.all_to_all(sent, ('x', 'l'), 0, 0, tiled=True)  15.9 us
    all_to_all x1, waiting for transfers between devices, local(): moved = lax.all_to_all(sent, ('x', 'l'), 0, 0, tiled=True)  9.1 us
    all_gather x1, blocking collectives, local(): pooled = lax.all_gather(pooled, 'c', axis=0, tiled=True)  6.01 us
    all_gather x1, blocking collectives, local(): wide = lax.all_gather(part, 'c', axis=0, tiled=True)  5.9 us
    all_gather x1, blocking collectives, local(): lax.all_gather(moved.reshape(tokens, units + LANES), 'c', axis=0, tiled=T...  3.71 us
  transfers between devices with their start and end apart: 1, of which 1 were waited for; matrix products, arithmetic and copies ran while one was open for 2% of the time, Pallas kernels for 1%

profile of v8, /device:TPU:1, one launch (start us, length us, event | category | flops | bytes accessed | tf_op | source)
XLA Modules:
  0.0 144.4 jit_solution(7233313044611856450)
XLA Ops:
  0.6 1.9 %shard_map.94 = bf16[32,4,1152]{2,1,0:T(4,128)(2,1)} custom-call(bf16[128,1024]{1,0:T(8,128)(2,1)} %bitcast.11, s32[1,128]{1,0:T(1,128)} %order_ref.3, f32[1,128]{1,0:T(1,128)} %cot_ref.1), custom_call_target="tpu_custom_call" | custom-call | tf_op jit(solution)/shard_map/pallas_call | solution.py:274
  2.5 15.9 %all-to-all-start = ((bf16[32,4,1152]{2,1,0:T(4,128)(2,1)}), bf16[32,4,1152]{2,1,0:T(4,128)(2,1)S(1)}, u32[]{:S(2)}, u32[]{:S(2)}) async-start(bf16[32,4,1152]{2,1,0:T(4,128)(2,1)} %shard_map.94), calls=%async_computation | async-start | bytes 589824 | tf_op jit(solution)/shard_map/all_to_all | solution.py:277
  18.5 0.7 broadcast_in_dim.11.bias_ref
  19.2 2.0 %slice.3.weight_ref = bf16[1024,1408]{1,0:T(8,128)(2,1)S(1)} slice(bf16[1024,1536]{1,0:T(8,128)(2,1)} %rest_ref.1), slice={[0:1024], [0:1408]} | slice | bytes 5767168 | tf_op jit(solution)/shard_map/slice | solution.py:302
  21.2 2.2 %shard_map.95 = bf16[128,1536]{1,0:T(8,128)(2,1)} custom-call(bf16[256,1536]{1,0:T(8,128)(2,1)} %bitcast.10, s32[1,256]{1,0:T(1,128)} %slot_ref.1), custom_call_target="tpu_custom_call" | custom-call | tf_op jit(solution)/shard_map/pallas_call | solution.py:278
  23.4 6.0 %all_gather.10.pooled_ref = bf16[256,1536]{1,0:T(8,128)(2,1)} all-gather(bf16[128,1536]{1,0:T(8,128)(2,1)} %shard_map.95), channel_id=1, replica_groups=mesh['y'=4,'h'=4,'x'=4,'l'=8,'c'=2] {'c'}, dimensions={0}, use_global_device_ids=true | all-gather | bytes 1179648 | tf_op jit(solution)/shard_map/all_gather | solution.py:281
  29.4 9.1 %all-to-all-done = bf16[32,4,1152]{2,1,0:T(4,128)(2,1)S(1)} async-done(((bf16[32,4,1152]{2,1,0:T(4,128)(2,1)}), bf16[32,4,1152]{2,1,0:T(4,128)(2,1)S(1)}, u32[]{:S(2)}, u32[]{:S(2)}) %all-to-all-start) | async-done | bytes 294944 | tf_op jit(solution)/shard_map/all_to_all | solution.py:277
  38.5 0.1 reshape.15
  38.5 3.7 %all_gather.9.both_ref = bf16[256,1152]{1,0:T(8,128)(2,1)S(1)} all-gather(bf16[128,1152]{1,0:T(8,128)(2,1)S(1)} %reshape.15), channel_id=1, replica_groups=mesh['y'=4,'h'=4,'x'=4,'l'=8,'c'=2] {'c'}, dimensions={0}, use_global_device_ids=true | all-gather | bytes 884736 | tf_op jit(solution)/shard_map/all_gather | solution.py:284
  42.2 3.2 %shard_map.96 = (bf16[16,400,128]{2,1,0:T(8,128)(2,1)S(1)}, f32[40,128]{1,0:T(8,128)S(1)}) custom-call(s32[1]{0:T(128)} %bitcast.core_ref, s32[1]{0:T(128)} %bitcast.1.high_ref, bf16[256,1152]{1,0:T(8,128)(2,1)S(1)} %all_gather.9.both_ref, bf16[256,1536]{1,0:T(8,128)(2,1)} %all_gather.10.pooled_ref, bf16[1024,1408]{1,0:T(8,128)(2,1)S(1)} %slice.3.weight_ref, ...), custom_call_target="tpu_custom_call" | custom-call | tf_op jit(solution)/shard_map/pallas_call | solution.py:287
  45.4 0.0 copy-start
  45.4 27.1 %all_to_all.20.part_ref = bf16[16,400,128]{2,1,0:T(8,128)(2,1)S(1)} all-to-all(bf16[16,400,128]{2,1,0:T(8,128)(2,1)S(1)} %get-tuple-element.10), channel_id=1, replica_groups=mesh['y'=4,'h'=4,'x'=4,'l'=8,'c'=2] {'x','y'}, dimensions={0} | all-to-all | bytes 3276800 | tf_op jit(solution)/shard_map/all_to_all | solution.py:304
  72.5 0.3 shard_map.97
  72.8 42.8 %all_to_all.21.part_ref = bf16[32,16,128]{2,1,0:T(8,128)(2,1)S(1)} all-to-all(bf16[32,16,128]{2,1,0:T(8,128)(2,1)S(1)} %bitcast.9), channel_id=1, replica_groups=mesh['y'=4,'h'=4,'x'=4,'l'=8,'c'=2] {'l','h'}, dimensions={0} | all-to-all | bytes 262144 | tf_op jit(solution)/shard_map/all_to_all | solution.py:313
  115.6 0.1 shard_map.98
  115.7 21.8 %all_to_all.22 = bf16[32,16,128]{2,1,0:T(8,128)(2,1)S(1)} all-to-all(bf16[32,16,128]{2,1,0:T(8,128)(2,1)S(1)} %shard_map.98), channel_id=1, replica_groups=mesh['y'=4,'h'=4,'x'=4,'l'=8,'c'=2] {'x','l'}, dimensions={0} | all-to-all | bytes 262144 | tf_op jit(solution)/shard_map/all_to_all | solution.py:315
  137.5 5.9 %all_gather.11.both_ref = bf16[1024,128]{1,0:T(8,128)(2,1)S(1)} all-gather(bf16[512,128]{1,0:T(8,128)(2,1)S(1)} %bitcast.7), channel_id=1, replica_groups=mesh['y'=4,'h'=4,'x'=4,'l'=8,'c'=2] {'c'}, dimensions={0}, use_global_device_ids=true | all-gather | bytes 393216 | tf_op jit(solution)/shard_map/all_gather | solution.py:316
  143.4 0.0 copy-done
  143.4 1.0 shard_map.99
Async XLA Ops:
  2.5 35.9 %all-to-all-start = ((bf16[32,4,1152]{2,1,0:T(4,128)(2,1)}), bf16[32,4,1152]{2,1,0:T(4,128)(2,1)S(1)}, u32[]{:S(2)}, u32[]{:S(2)}) async-start(bf16[32,4,1152]{2,1,0:T(4,128)(2,1)} %shard_map.94), calls=%async_computation | async-start | bytes 589824 | tf_op jit(solution)/shard_map/all_to_all | solution.py:277
  45.4 98.0 %copy-start = (s32[1,128]{1,0:T(1,128)S(1)}, s32[1,128]{1,0:T(1,128)}, u32[]{:S(2)}) copy-start(s32[1,128]{1,0:T(1,128)} %order_ref.3) | copy-start | bytes 1540

commit v9 on v8

--- a/solution.py
+++ b/solution.py
@@ -71,9 +71,26 @@
     pooled_ref[...] = (totals / counts).astype(BF)
 
 
+def target_kernel(dims, pooled_ref, target_ref):
+    y_n, h_n, x_n, l_n, c_n, two = dims
+    near, per = x_n * l_n, c_n * two
+    tokens = pooled_ref.shape[0]
+    single = tokens // c_n
+    row = iota((tokens, tokens), 0)
+    wanted = (
+        (row // two) % c_n * single + row // single * (near * two) + row // per % near * two + row % two
+    )
+    turn = jnp.where(wanted == iota((tokens, tokens), 1), 1.0, 0.0).astype(BF)
+    step = 256
+    for at in range(0, pooled_ref.shape[1], step):
+        cut = slice(at, at + step)
+        t = jnp.dot(turn, pooled_ref[:, cut], preferred_element_type=F32)
+        target_ref[:, cut] = t.astype(BF)
+
+
 def middle_kernel(
-    dims, core_ref, high_ref, both_ref, pooled_ref, weight_ref, rest_ref, bias_ref, part_ref, back_ref,
-    proj, target, grads, held, pooled, sems
+    dims, core_ref, high_ref, both_ref, target_ref, weight_ref, rest_ref, bias_ref, part_ref, back_ref,
+    proj, grads, held, target, sems
 ):
     y_n, h_n, x_n, l_n, c_n, two = dims
     near, per = x_n * l_n, c_n * two
@@ -81,18 +98,13 @@
     first = weight_ref.shape[1]
     fetch_rest = pltpu.make_async_copy(rest_ref.at[:, pl.ds(first, LANES)], held, sems.at[1])
     fetch_rest.start()
-    fetch = pltpu.make_async_copy(pooled_ref, pooled, sems.at[0])
+    fetch = pltpu.make_async_copy(target_ref, target, sems.at[0])
     fetch.start()
     acts = both_ref[:, :units]
     width = rest_ref.shape[1]
     half = width // c_n
     single = tokens // c_n
     core = core_ref[0]
-    row = iota((tokens, tokens), 0)
-    wanted = (
-        (row // two) % c_n * single + row // single * (near * two) + row // per % near * two + row % two
-    )
-    turn = jnp.where(wanted == iota((tokens, tokens), 1), 1.0, 0.0).astype(BF)
     step = 256
     s_pp = jnp.zeros((tokens, 1), F32)
     s_tt = jnp.zeros((tokens, 1), F32)
@@ -110,8 +122,7 @@
     fetch.wait()
     for at in range(0, width, step):
         cut = slice(at, at + step)
-        t = jnp.dot(turn, pooled[:, cut], preferred_element_type=F32)
-        target[:, cut] = t
+        t = target[:, cut].astype(F32)
         s_tt = s_tt + jnp.sum(t * t, axis=1, keepdims=True)
         s_pt = s_pt + jnp.sum(proj[:, cut] * t, axis=1, keepdims=True)
     inv_proj = lax.rsqrt(s_pp + 1e-06)
@@ -125,7 +136,7 @@
     tail_row = iota((TAIL, step), 0)
     main = part_ref.shape[1] - TAIL
     for at in range(0, width, step):
-        g = cot * (target[:, at : at + step] * scale_t - scale_p * proj[:, at : at + step])
+        g = cot * (target[:, at : at + step].astype(F32) * scale_t - scale_p * proj[:, at : at + step])
         g = g.astype(BF)
         inside = at % half
         grads[at // half, :, inside : inside + step] = g
@@ -143,7 +154,9 @@
     high, low = split_two(cosine)
     spot = iota((tokens, LANES), 0) % per == lane
     owner = iota((near, tokens), 1) - core * single
-    gather = jnp.where((owner >= 0) & (owner < single) & (owner // per == iota((near, tokens), 0)), 1.0, 0.0)
+    chip = iota((near, tokens), 0)
+    chip = chip % x_n * l_n + chip // x_n
+    gather = jnp.where((owner >= 0) & (owner < single) & (owner // per == chip), 1.0, 0.0)
     gather = gather.astype(BF)
     back = jnp.zeros((near, LANES), F32)
     for term in (high, low):
@@ -230,14 +243,15 @@
         for x in range(x_n):
             for k in range(pairs):
                 for r in range(LINE_ROWS):
-                    start = (c * near + x * l_n) * group + k * LINE_ROWS + r
+                    start = (c * near + x) * group + k * LINE_ROWS + r
                     to = (x * LINE_ROWS + r) * l_n
                     at = c * half + k * LANES
-                    weight_ref[to : to + l_n, at : at + LANES] = wide[pl.ds(start, l_n, stride=group), :]
+                    weight_ref[to : to + l_n, at : at + LANES] = wide[pl.ds(start, l_n, stride=x_n * group), :]
     cosines = narrow[pl.ds(group - 2, near, stride=group), :] + narrow[pl.ds(group - 1, near, stride=group), :]
     order = order_ref[...]
     tokens = order.shape[1]
-    base = iota((near, tokens), 0) * per
+    chip = iota((near, tokens), 0)
+    base = (chip % x_n * l_n + chip // x_n) * per
     total = jnp.zeros((near, tokens), F32)
     for i in range(per):
         total = total + jnp.where(order == base + i, cosines[:, i : i + 1], 0.0)
@@ -247,7 +261,7 @@
     offset = back_ref[near:, :cols].astype(I32)[0:1] * cols
     out = jnp.zeros((8, cols), F32)
     for b in range(blocks):
-        start = b * l_n * group + lines
+        start = b * group + lines
         pick = iota((LANES, cols), 0) + b * LANES == iota((LANES, cols), 1) + offset
         pick = jnp.where(pick, 1.0, 0.0).astype(BF)
         for r in range(2):
@@ -279,7 +293,10 @@
         functools.partial(pool_kernel, dims), shape((tokens, width), BF), [VMEM] * 2, limit=60
     )(patches, slots)
     pooled = lax.all_gather(pooled, "c", axis=0, tiled=True)
-    pooled = pltpu.with_memory_space_constraint(pooled, pltpu.HBM)
+    target = call(
+        functools.partial(target_kernel, dims), shape((c_n * tokens, width), BF), [VMEM], limit=60
+    )(pooled)
+    target = pltpu.with_memory_space_constraint(target, pltpu.HBM)
 
     both = lax.all_gather(moved.reshape(tokens, units + LANES), "c", axis=0, tiled=True)
     rows = units // (y_n * x_n)
@@ -293,13 +310,12 @@
         [SMEM] * 2 + [VMEM, HBM, VMEM, HBM, VMEM],
         [
             pltpu.VMEM((c_n * tokens, width), F32),
-            pltpu.VMEM((c_n * tokens, width), F32),
             pltpu.VMEM((c_n, c_n * tokens, half), BF),
             pltpu.VMEM((units, LANES), BF),
             pltpu.VMEM((c_n * tokens, width), BF),
             pltpu.SemaphoreType.DMA((2,)),
         ],
-    )(core, high, both, pooled, weight[:, : width - LANES], pltpu.with_memory_space_constraint(weight, pltpu.HBM), bias[None, :])
+    )(core, high, both, target, weight[:, : width - LANES], pltpu.with_memory_space_constraint(weight, pltpu.HBM), bias[None, :])
 
     part = lax.all_to_all(part, ("x", "y"), 0, 0, tiled=True)
     spots = h_n * l_n
@@ -312,7 +328,7 @@
     part, back = lax.optimization_barrier((part, back))
     part = lax.all_to_all(part.reshape(spots, TAIL, LANES), ("l", "h"), 0, 0, tiled=True)
     part = call(functools.partial(line_kernel, lines), shape((near, TAIL, LANES), BF), [VMEM] * 2)(part, back)
-    part = lax.all_to_all(part, ("x", "l"), 0, 0, tiled=True).reshape(near * TAIL, LANES)
+    part = lax.all_to_all(part, ("l", "x"), 0, 0, tiled=True).reshape(near * TAIL, LANES)
     wide = lax.all_gather(part, "c", axis=0, tiled=True)
     cos_sim, weight_grad, bias_grad = call(
         functools.partial(unpack_kernel, dims),

time: 145 us -> 145 us (level)
  waiting for transfers between devices: 9.1 us -> 6.69 us
  Pallas kernels: 8.57 us -> 10.9 us
    all_to_all x1, waiting for transfers between devices: 9.1 us -> 6.69 us  [local(): moved = lax.all_to_all(sent, ('x', 'l'), 0, 0, tiled=True)]
    pallas_call x0 -> x1, Pallas kernels: none -> 2.39 us  [local(): call(functools.partial(target_kernel, dims), shape((c_n * tokens, width),...]
  transfers between devices with their start and end apart: 1 -> 1, of which waited for: 1 -> 1; matrix products, arithmetic and copies ran while one was open for 2% -> 2% of each run, Pallas kernels for 1% -> 3%
where the time goes in v9:
time: 145 us
  blocking collectives  108 us (74%)
  starting transfers between devices  15.9 us (11%)
  Pallas kernels  10.9 us (8%)
  waiting for transfers between devices  6.69 us (5%)
  local copies, waits for them, and re-layouts  2.81 us (2%)
    all_to_all x1, blocking collectives, local(): lax.all_to_all(part.reshape(spots, TAIL, LANES), ('l', 'h'), 0, 0, tiled=...  42.8 us
    all_to_all x1, blocking collectives, local(): part = lax.all_to_all(part, ('x', 'y'), 0, 0, tiled=True)  27.1 us
    all_to_all x1, blocking collectives, local(): lax.all_to_all(part, ('l', 'x'), 0, 0, tiled=True)  22.2 us
    all_to_all x1, starting transfers between devices, local(): moved = lax.all_to_all(sent, ('x', 'l'), 0, 0, tiled=True)  15.9 us
    all_to_all x1, waiting for transfers between devices, local(): moved = lax.all_to_all(sent, ('x', 'l'), 0, 0, tiled=True)  6.69 us
    all_gather x1, blocking collectives, local(): pooled = lax.all_gather(pooled, 'c', axis=0, tiled=True)  6.02 us
    all_gather x1, blocking collectives, local(): wide = lax.all_gather(part, 'c', axis=0, tiled=True)  5.9 us
    all_gather x1, blocking collectives, local(): lax.all_gather(moved.reshape(tokens, units + LANES), 'c', axis=0, tiled=T...  3.71 us
  transfers between devices with their start and end apart: 1, of which 1 were waited for; matrix products, arithmetic and copies ran while one was open for 2% of the time, Pallas kernels for 3%

profile of v9, /device:TPU:1, one launch (start us, length us, event | category | flops | bytes accessed | tf_op | source)
XLA Modules:
  0.0 144.7 jit_solution(7106342046335279207)
XLA Ops:
  0.6 1.9 %shard_map.94 = bf16[32,4,1152]{2,1,0:T(4,128)(2,1)} custom-call(bf16[128,1024]{1,0:T(8,128)(2,1)} %bitcast.11, s32[1,128]{1,0:T(1,128)} %order_ref.3, f32[1,128]{1,0:T(1,128)} %cot_ref.1), custom_call_target="tpu_custom_call" | custom-call | tf_op jit(solution)/shard_map/pallas_call | solution.py:288
  2.5 15.9 %all-to-all-start = ((bf16[32,4,1152]{2,1,0:T(4,128)(2,1)}), bf16[32,4,1152]{2,1,0:T(4,128)(2,1)S(1)}, u32[]{:S(2)}, u32[]{:S(2)}) async-start(bf16[32,4,1152]{2,1,0:T(4,128)(2,1)} %shard_map.94), calls=%async_computation | async-start | bytes 589824 | tf_op jit(solution)/shard_map/all_to_all | solution.py:291
  18.5 0.7 broadcast_in_dim.11.bias_ref
  19.2 2.2 %shard_map.95 = bf16[128,1536]{1,0:T(8,128)(2,1)} custom-call(bf16[256,1536]{1,0:T(8,128)(2,1)} %bitcast.10, s32[1,256]{1,0:T(1,128)} %slot_ref.1), custom_call_target="tpu_custom_call" | custom-call | tf_op jit(solution)/shard_map/pallas_call | solution.py:292
  21.3 6.0 %all_gather.10.pooled_ref = bf16[256,1536]{1,0:T(8,128)(2,1)} all-gather(bf16[128,1536]{1,0:T(8,128)(2,1)} %shard_map.95), channel_id=1, replica_groups=mesh['y'=4,'h'=4,'x'=4,'l'=8,'c'=2] {'c'}, dimensions={0}, use_global_device_ids=true | all-gather | bytes 1179648 | tf_op jit(solution)/shard_map/all_gather | solution.py:295
  27.3 2.4 %shard_map.96.target_ref = bf16[256,1536]{1,0:T(8,128)(2,1)} custom-call(bf16[256,1536]{1,0:T(8,128)(2,1)} %all_gather.10.pooled_ref), custom_call_target="tpu_custom_call" | custom-call | tf_op jit(solution)/shard_map/pallas_call | solution.py:296
  29.7 2.0 %slice.3.weight_ref = bf16[1024,1408]{1,0:T(8,128)(2,1)S(1)} slice(bf16[1024,1536]{1,0:T(8,128)(2,1)} %rest_ref.1), slice={[0:1024], [0:1408]} | slice | bytes 5767168 | tf_op jit(solution)/shard_map/slice | solution.py:318
  31.8 6.7 %all-to-all-done = bf16[32,4,1152]{2,1,0:T(4,128)(2,1)S(1)} async-done(((bf16[32,4,1152]{2,1,0:T(4,128)(2,1)}), bf16[32,4,1152]{2,1,0:T(4,128)(2,1)S(1)}, u32[]{:S(2)}, u32[]{:S(2)}) %all-to-all-start) | async-done | bytes 294944 | tf_op jit(solution)/shard_map/all_to_all | solution.py:291
  38.5 0.1 reshape.15
  38.5 3.7 %all_gather.9.both_ref = bf16[256,1152]{1,0:T(8,128)(2,1)S(1)} all-gather(bf16[128,1152]{1,0:T(8,128)(2,1)S(1)} %reshape.15), channel_id=1, replica_groups=mesh['y'=4,'h'=4,'x'=4,'l'=8,'c'=2] {'c'}, dimensions={0}, use_global_device_ids=true | all-gather | bytes 884736 | tf_op jit(solution)/shard_map/all_gather | solution.py:301
  42.2 3.0 %shard_map.97 = (bf16[16,400,128]{2,1,0:T(8,128)(2,1)S(1)}, f32[40,128]{1,0:T(8,128)S(1)}) custom-call(s32[1]{0:T(128)} %bitcast.core_ref, s32[1]{0:T(128)} %bitcast.1.high_ref, bf16[256,1152]{1,0:T(8,128)(2,1)S(1)} %all_gather.9.both_ref, bf16[256,1536]{1,0:T(8,128)(2,1)} %shard_map.96.target_ref, bf16[1024,1408]{1,0:T(8,128)(2,1)S(1)} %slice.3.weight_ref, ...), custom_call_target="tpu_custom_call" | custom-call | tf_op jit(solution)/shard_map/pallas_call | solution.py:304
  45.3 0.0 copy-start
  45.3 27.1 %all_to_all.20.part_ref = bf16[16,400,128]{2,1,0:T(8,128)(2,1)S(1)} all-to-all(bf16[16,400,128]{2,1,0:T(8,128)(2,1)S(1)} %get-tuple-element.10), channel_id=1, replica_groups=mesh['y'=4,'h'=4,'x'=4,'l'=8,'c'=2] {'x','y'}, dimensions={0} | all-to-all | bytes 3276800 | tf_op jit(solution)/shard_map/all_to_all | solution.py:320
  72.4 0.3 shard_map.98
  72.7 42.8 %all_to_all.21.part_ref = bf16[32,16,128]{2,1,0:T(8,128)(2,1)S(1)} all-to-all(bf16[32,16,128]{2,1,0:T(8,128)(2,1)S(1)} %bitcast.9), channel_id=1, replica_groups=mesh['y'=4,'h'=4,'x'=4,'l'=8,'c'=2] {'l','h'}, dimensions={0} | all-to-all | bytes 262144 | tf_op jit(solution)/shard_map/all_to_all | solution.py:329
  115.5 0.1 shard_map.99
  115.5 22.2 %all_to_all.22 = bf16[32,16,128]{2,1,0:T(8,128)(2,1)S(1)} all-to-all(bf16[32,16,128]{2,1,0:T(8,128)(2,1)S(1)} %shard_map.99), channel_id=1, replica_groups=mesh['y'=4,'h'=4,'x'=4,'l'=8,'c'=2] {'l','x'}, dimensions={0} | all-to-all | bytes 262144 | tf_op jit(solution)/shard_map/all_to_all | solution.py:331
  137.7 5.9 %all_gather.11.both_ref = bf16[1024,128]{1,0:T(8,128)(2,1)S(1)} all-gather(bf16[512,128]{1,0:T(8,128)(2,1)S(1)} %bitcast.7), channel_id=1, replica_groups=mesh['y'=4,'h'=4,'x'=4,'l'=8,'c'=2] {'c'}, dimensions={0}, use_global_device_ids=true | all-gather | bytes 393216 | tf_op jit(solution)/shard_map/all_gather | solution.py:332
  143.6 0.0 copy-done
  143.6 1.1 shard_map.100
Async XLA Ops:
  2.5 35.9 %all-to-all-start = ((bf16[32,4,1152]{2,1,0:T(4,128)(2,1)}), bf16[32,4,1152]{2,1,0:T(4,128)(2,1)S(1)}, u32[]{:S(2)}, u32[]{:S(2)}) async-start(bf16[32,4,1152]{2,1,0:T(4,128)(2,1)} %shard_map.94), calls=%async_computation | async-start | bytes 589824 | tf_op jit(solution)/shard_map/all_to_all | solution.py:291
  45.3 98.3 %copy-start = (s32[1,128]{1,0:T(1,128)S(1)}, s32[1,128]{1,0:T(1,128)}, u32[]{:S(2)}) copy-start(s32[1,128]{1,0:T(1,128)} %order_ref.3) | copy-start | bytes 1540

commit v10 on v8

--- a/solution.py
+++ b/solution.py
@@ -134,11 +134,11 @@
         tail = jnp.where(tail_row == 0, high, jnp.where(tail_row == 1, total - high, 0.0)).astype(BF)
         for k in range(step // LANES):
             block = at // LANES + k
-            piece = block % y_blocks * y_n + block // y_blocks
+            piece = block // y_blocks * x_n + block % y_blocks
             part_ref[piece, main:, :] = tail[:, k * LANES : (k + 1) * LANES]
     for y in range(y_n):
         for x in range(y_blocks, x_n):
-            part_ref[x * y_n + y, main:, :] = jnp.zeros((TAIL, LANES), BF)
+            part_ref[y * x_n + x, main:, :] = jnp.zeros((TAIL, LANES), BF)
     lane = iota((tokens, LANES), 1)
     high, low = split_two(cosine)
     spot = iota((tokens, LANES), 0) % per == lane
@@ -163,7 +163,7 @@
                 start = (h * x_n + x) * chunk
                 for k in range(half // LANES):
                     to = (k * h_n + h) * chunk
-                    part_ref[x * y_n + y, to : to + chunk, :] = product[
+                    part_ref[y * x_n + x, to : to + chunk, :] = product[
                         start : start + chunk, k * LANES : (k + 1) * LANES
                     ]
 
@@ -189,7 +189,7 @@
         for h in range(h_n):
             for r in range(LINE_ROWS):
                 at = (h * LINE_ROWS + r) * l_n
-                spread[pl.ds(h * group + k * LINE_ROWS + r, l_n, stride=h_n * group), :] = total[at : at + l_n]
+                spread[pl.ds(h * l_n * group + k * LINE_ROWS + r, l_n, stride=group), :] = total[at : at + l_n]
     tail = summed(main, TAIL)
     bias = tail[0:1] + tail[1:2]
     high = bias.astype(BF).astype(F32)
@@ -301,7 +301,7 @@
         ],
     )(core, high, both, pooled, weight[:, : width - LANES], pltpu.with_memory_space_constraint(weight, pltpu.HBM), bias[None, :])
 
-    part = lax.all_to_all(part, ("x", "y"), 0, 0, tiled=True)
+    part = lax.all_to_all(part, ("y", "x"), 0, 0, tiled=True)
     spots = h_n * l_n
     part = call(
         functools.partial(plane_kernel, dims),
@@ -310,7 +310,7 @@
         [pltpu.VMEM((spots * TAIL, LANES), F32)],
     )(part)
     part, back = lax.optimization_barrier((part, back))
-    part = lax.all_to_all(part.reshape(spots, TAIL, LANES), ("l", "h"), 0, 0, tiled=True)
+    part = lax.all_to_all(part.reshape(spots, TAIL, LANES), ("h", "l"), 0, 0, tiled=True)
     part = call(functools.partial(line_kernel, lines), shape((near, TAIL, LANES), BF), [VMEM] * 2)(part, back)
     part = lax.all_to_all(part, ("x", "l"), 0, 0, tiled=True).reshape(near * TAIL, LANES)
     wide = lax.all_gather(part, "c", axis=0, tiled=True)

time: 145 us -> 145 us (level)
    all_to_all x2, blocking collectives: 69.9 us -> 75.5 us  [the longest x1 48.5 us: local(): lax.all_to_all(part.reshape(spots, TAIL, LANES), ('h', 'l'), 0, 0, tiled=...]
    all_to_all x1, blocking collectives: 21.8 us -> 16.6 us  [local(): lax.all_to_all(part, ('x', 'l'), 0, 0, tiled=True)]
where the time goes in v10:
time: 145 us
  blocking collectives  108 us (74%)
  starting transfers between devices  15.9 us (11%)
  waiting for transfers between devices  9.1 us (6%)
  Pallas kernels  8.53 us (6%)
  local copies, waits for them, and re-layouts  2.81 us (2%)
    all_to_all x1, blocking collectives, local(): lax.all_to_all(part.reshape(spots, TAIL, LANES), ('h', 'l'), 0, 0, tiled=...  48.5 us
    all_to_all x1, blocking collectives, local(): part = lax.all_to_all(part, ('y', 'x'), 0, 0, tiled=True)  27 us
    all_to_all x1, blocking collectives, local(): lax.all_to_all(part, ('x', 'l'), 0, 0, tiled=True)  16.6 us
    all_to_all x1, starting transfers between devices, local(): moved = lax.all_to_all(sent, ('x', 'l'), 0, 0, tiled=True)  15.9 us
    all_to_all x1, waiting for transfers between devices, local(): moved = lax.all_to_all(sent, ('x', 'l'), 0, 0, tiled=True)  9.1 us
    all_gather x1, blocking collectives, local(): pooled = lax.all_gather(pooled, 'c', axis=0, tiled=True)  6.01 us
    all_gather x1, blocking collectives, local(): wide = lax.all_gather(part, 'c', axis=0, tiled=True)  5.72 us
    all_gather x1, blocking collectives, local(): lax.all_gather(moved.reshape(tokens, units + LANES), 'c', axis=0, tiled=T...  3.71 us
  transfers between devices with their start and end apart: 1, of which 1 were waited for; matrix products, arithmetic and copies ran while one was open for 2% of the time, Pallas kernels for 1%

profile of v10, /device:TPU:1, one launch (start us, length us, event | category | flops | bytes accessed | tf_op | source)
XLA Modules:
  0.0 144.5 jit_solution(6965116750290987581)
XLA Ops:
  0.6 1.9 %shard_map.94 = bf16[32,4,1152]{2,1,0:T(4,128)(2,1)} custom-call(bf16[128,1024]{1,0:T(8,128)(2,1)} %bitcast.11, s32[1,128]{1,0:T(1,128)} %order_ref.3, f32[1,128]{1,0:T(1,128)} %cot_ref.1), custom_call_target="tpu_custom_call" | custom-call | tf_op jit(solution)/shard_map/pallas_call | solution.py:274
  2.5 15.9 %all-to-all-start = ((bf16[32,4,1152]{2,1,0:T(4,128)(2,1)}), bf16[32,4,1152]{2,1,0:T(4,128)(2,1)S(1)}, u32[]{:S(2)}, u32[]{:S(2)}) async-start(bf16[32,4,1152]{2,1,0:T(4,128)(2,1)} %shard_map.94), calls=%async_computation | async-start | bytes 589824 | tf_op jit(solution)/shard_map/all_to_all | solution.py:277
  18.5 0.7 broadcast_in_dim.11.bias_ref
  19.2 2.0 %slice.3.weight_ref = bf16[1024,1408]{1,0:T(8,128)(2,1)S(1)} slice(bf16[1024,1536]{1,0:T(8,128)(2,1)} %rest_ref.1), slice={[0:1024], [0:1408]} | slice | bytes 5767168 | tf_op jit(solution)/shard_map/slice | solution.py:302
  21.2 2.2 %shard_map.95 = bf16[128,1536]{1,0:T(8,128)(2,1)} custom-call(bf16[256,1536]{1,0:T(8,128)(2,1)} %bitcast.10, s32[1,256]{1,0:T(1,128)} %slot_ref.1), custom_call_target="tpu_custom_call" | custom-call | tf_op jit(solution)/shard_map/pallas_call | solution.py:278
  23.4 6.0 %all_gather.10.pooled_ref = bf16[256,1536]{1,0:T(8,128)(2,1)} all-gather(bf16[128,1536]{1,0:T(8,128)(2,1)} %shard_map.95), channel_id=1, replica_groups=mesh['y'=4,'h'=4,'x'=4,'l'=8,'c'=2] {'c'}, dimensions={0}, use_global_device_ids=true | all-gather | bytes 1179648 | tf_op jit(solution)/shard_map/all_gather | solution.py:281
  29.4 9.1 %all-to-all-done = bf16[32,4,1152]{2,1,0:T(4,128)(2,1)S(1)} async-done(((bf16[32,4,1152]{2,1,0:T(4,128)(2,1)}), bf16[32,4,1152]{2,1,0:T(4,128)(2,1)S(1)}, u32[]{:S(2)}, u32[]{:S(2)}) %all-to-all-start) | async-done | bytes 294944 | tf_op jit(solution)/shard_map/all_to_all | solution.py:277
  38.5 0.1 reshape.15
  38.5 3.7 %all_gather.9.both_ref = bf16[256,1152]{1,0:T(8,128)(2,1)S(1)} all-gather(bf16[128,1152]{1,0:T(8,128)(2,1)S(1)} %reshape.15), channel_id=1, replica_groups=mesh['y'=4,'h'=4,'x'=4,'l'=8,'c'=2] {'c'}, dimensions={0}, use_global_device_ids=true | all-gather | bytes 884736 | tf_op jit(solution)/shard_map/all_gather | solution.py:284
  42.2 3.2 %shard_map.96 = (bf16[16,400,128]{2,1,0:T(8,128)(2,1)S(1)}, f32[40,128]{1,0:T(8,128)S(1)}) custom-call(s32[1]{0:T(128)} %bitcast.core_ref, s32[1]{0:T(128)} %bitcast.1.high_ref, bf16[256,1152]{1,0:T(8,128)(2,1)S(1)} %all_gather.9.both_ref, bf16[256,1536]{1,0:T(8,128)(2,1)} %all_gather.10.pooled_ref, bf16[1024,1408]{1,0:T(8,128)(2,1)S(1)} %slice.3.weight_ref, ...), custom_call_target="tpu_custom_call" | custom-call | tf_op jit(solution)/shard_map/pallas_call | solution.py:287
  45.4 0.0 copy-start
  45.4 27.0 %all_to_all.20.part_ref = bf16[16,400,128]{2,1,0:T(8,128)(2,1)S(1)} all-to-all(bf16[16,400,128]{2,1,0:T(8,128)(2,1)S(1)} %get-tuple-element.10), channel_id=1, replica_groups=mesh['y'=4,'h'=4,'x'=4,'l'=8,'c'=2] {'y','x'}, dimensions={0} | all-to-all | bytes 3276800 | tf_op jit(solution)/shard_map/all_to_all | solution.py:304
  72.4 0.3 shard_map.97
  72.7 48.5 %all_to_all.21.part_ref = bf16[32,16,128]{2,1,0:T(8,128)(2,1)S(1)} all-to-all(bf16[32,16,128]{2,1,0:T(8,128)(2,1)S(1)} %bitcast.9), channel_id=1, replica_groups=mesh['y'=4,'h'=4,'x'=4,'l'=8,'c'=2] {'h','l'}, dimensions={0} | all-to-all | bytes 262144 | tf_op jit(solution)/shard_map/all_to_all | solution.py:313
  121.2 0.1 shard_map.98
  121.2 16.6 %all_to_all.22 = bf16[32,16,128]{2,1,0:T(8,128)(2,1)S(1)} all-to-all(bf16[32,16,128]{2,1,0:T(8,128)(2,1)S(1)} %shard_map.98), channel_id=1, replica_groups=mesh['y'=4,'h'=4,'x'=4,'l'=8,'c'=2] {'x','l'}, dimensions={0} | all-to-all | bytes 262144 | tf_op jit(solution)/shard_map/all_to_all | solution.py:315
  137.8 5.7 %all_gather.11.both_ref = bf16[1024,128]{1,0:T(8,128)(2,1)S(1)} all-gather(bf16[512,128]{1,0:T(8,128)(2,1)S(1)} %bitcast.7), channel_id=1, replica_groups=mesh['y'=4,'h'=4,'x'=4,'l'=8,'c'=2] {'c'}, dimensions={0}, use_global_device_ids=true | all-gather | bytes 393216 | tf_op jit(solution)/shard_map/all_gather | solution.py:316
  143.6 0.0 copy-done
  143.6 1.0 shard_map.99
Async XLA Ops:
  2.5 35.9 %all-to-all-start = ((bf16[32,4,1152]{2,1,0:T(4,128)(2,1)}), bf16[32,4,1152]{2,1,0:T(4,128)(2,1)S(1)}, u32[]{:S(2)}, u32[]{:S(2)}) async-start(bf16[32,4,1152]{2,1,0:T(4,128)(2,1)} %shard_map.94), calls=%async_computation | async-start | bytes 589824 | tf_op jit(solution)/shard_map/all_to_all | solution.py:277
  45.4 98.1 %copy-start = (s32[1,128]{1,0:T(1,128)S(1)}, s32[1,128]{1,0:T(1,128)}, u32[]{:S(2)}) copy-start(s32[1,128]{1,0:T(1,128)} %order_ref.3) | copy-start | bytes 1540

commit v11 on v9

--- a/solution.py
+++ b/solution.py
@@ -145,18 +145,16 @@
         tail = jnp.where(tail_row == 0, high, jnp.where(tail_row == 1, total - high, 0.0)).astype(BF)
         for k in range(step // LANES):
             block = at // LANES + k
-            piece = block % y_blocks * y_n + block // y_blocks
+            piece = block // y_blocks * x_n + block % y_blocks
             part_ref[piece, main:, :] = tail[:, k * LANES : (k + 1) * LANES]
     for y in range(y_n):
         for x in range(y_blocks, x_n):
-            part_ref[x * y_n + y, main:, :] = jnp.zeros((TAIL, LANES), BF)
+            part_ref[y * x_n + x, main:, :] = jnp.zeros((TAIL, LANES), BF)
     lane = iota((tokens, LANES), 1)
     high, low = split_two(cosine)
     spot = iota((tokens, LANES), 0) % per == lane
     owner = iota((near, tokens), 1) - core * single
-    chip = iota((near, tokens), 0)
-    chip = chip % x_n * l_n + chip // x_n
-    gather = jnp.where((owner >= 0) & (owner < single) & (owner // per == chip), 1.0, 0.0)
+    gather = jnp.where((owner >= 0) & (owner < single) & (owner // per == iota((near, tokens), 0)), 1.0, 0.0)
     gather = gather.astype(BF)
     back = jnp.zeros((near, LANES), F32)
     for term in (high, low):
@@ -176,7 +174,7 @@
                 start = (h * x_n + x) * chunk
                 for k in range(half // LANES):
                     to = (k * h_n + h) * chunk
-                    part_ref[x * y_n + y, to : to + chunk, :] = product[
+                    part_ref[y * x_n + x, to : to + chunk, :] = product[
                         start : start + chunk, k * LANES : (k + 1) * LANES
                     ]
 
@@ -202,7 +200,7 @@
         for h in range(h_n):
             for r in range(LINE_ROWS):
                 at = (h * LINE_ROWS + r) * l_n
-                spread[pl.ds(h * group + k * LINE_ROWS + r, l_n, stride=h_n * group), :] = total[at : at + l_n]
+                spread[pl.ds(h * l_n * group + k * LINE_ROWS + r, l_n, stride=group), :] = total[at : at + l_n]
     tail = summed(main, TAIL)
     bias = tail[0:1] + tail[1:2]
     high = bias.astype(BF).astype(F32)
@@ -243,15 +241,14 @@
         for x in range(x_n):
             for k in range(pairs):
                 for r in range(LINE_ROWS):
-                    start = (c * near + x) * group + k * LINE_ROWS + r
+                    start = (c * near + x * l_n) * group + k * LINE_ROWS + r
                     to = (x * LINE_ROWS + r) * l_n
                     at = c * half + k * LANES
-                    weight_ref[to : to + l_n, at : at + LANES] = wide[pl.ds(start, l_n, stride=x_n * group), :]
+                    weight_ref[to : to + l_n, at : at + LANES] = wide[pl.ds(start, l_n, stride=group), :]
     cosines = narrow[pl.ds(group - 2, near, stride=group), :] + narrow[pl.ds(group - 1, near, stride=group), :]
     order = order_ref[...]
     tokens = order.shape[1]
-    chip = iota((near, tokens), 0)
-    base = (chip % x_n * l_n + chip // x_n) * per
+    base = iota((near, tokens), 0) * per
     total = jnp.zeros((near, tokens), F32)
     for i in range(per):
         total = total + jnp.where(order == base + i, cosines[:, i : i + 1], 0.0)
@@ -261,7 +258,7 @@
     offset = back_ref[near:, :cols].astype(I32)[0:1] * cols
     out = jnp.zeros((8, cols), F32)
     for b in range(blocks):
-        start = b * group + lines
+        start = b * l_n * group + lines
         pick = iota((LANES, cols), 0) + b * LANES == iota((LANES, cols), 1) + offset
         pick = jnp.where(pick, 1.0, 0.0).astype(BF)
         for r in range(2):
@@ -317,7 +314,7 @@
         ],
     )(core, high, both, target, weight[:, : width - LANES], pltpu.with_memory_space_constraint(weight, pltpu.HBM), bias[None, :])
 
-    part = lax.all_to_all(part, ("x", "y"), 0, 0, tiled=True)
+    part = lax.all_to_all(part, ("y", "x"), 0, 0, tiled=True)
     spots = h_n * l_n
     part = call(
         functools.partial(plane_kernel, dims),
@@ -326,9 +323,9 @@
         [pltpu.VMEM((spots * TAIL, LANES), F32)],
     )(part)
     part, back = lax.optimization_barrier((part, back))
-    part = lax.all_to_all(part.reshape(spots, TAIL, LANES), ("l", "h"), 0, 0, tiled=True)
+    part = lax.all_to_all(part.reshape(spots, TAIL, LANES), ("h", "l"), 0, 0, tiled=True)
     part = call(functools.partial(line_kernel, lines), shape((near, TAIL, LANES), BF), [VMEM] * 2)(part, back)
-    part = lax.all_to_all(part, ("l", "x"), 0, 0, tiled=True).reshape(near * TAIL, LANES)
+    part = lax.all_to_all(part, ("x", "l"), 0, 0, tiled=True).reshape(near * TAIL, LANES)
     wide = lax.all_gather(part, "c", axis=0, tiled=True)
     cos_sim, weight_grad, bias_grad = call(
         functools.partial(unpack_kernel, dims),

time: 145 us -> 145 us (level)
  no operation moved by 1% of the time
where the time goes in v11:
time: 145 us; the launch traced here: 144 us
  blocking collectives  108 us (74%)
  starting transfers between devices  15.9 us (11%)
  Pallas kernels  10.8 us (7%)
  waiting for transfers between devices  6.69 us (5%)
  local copies, waits for them, and re-layouts  2.81 us (2%)
    all_to_all x1, blocking collectives, local(): lax.all_to_all(part.reshape(spots, TAIL, LANES), ('h', 'l'), 0, 0, tiled=...  48.5 us
    all_to_all x1, blocking collectives, local(): part = lax.all_to_all(part, ('y', 'x'), 0, 0, tiled=True)  27 us
    all_to_all x1, blocking collectives, local(): lax.all_to_all(part, ('x', 'l'), 0, 0, tiled=True)  16.6 us
    all_to_all x1, starting transfers between devices, local(): moved = lax.all_to_all(sent, ('x', 'l'), 0, 0, tiled=True)  15.9 us
    all_to_all x1, waiting for transfers between devices, local(): moved = lax.all_to_all(sent, ('x', 'l'), 0, 0, tiled=True)  6.69 us
    all_gather x1, blocking collectives, local(): pooled = lax.all_gather(pooled, 'c', axis=0, tiled=True)  6.02 us
    all_gather x1, blocking collectives, local(): wide = lax.all_gather(part, 'c', axis=0, tiled=True)  5.72 us
    all_gather x1, blocking collectives, local(): lax.all_gather(moved.reshape(tokens, units + LANES), 'c', axis=0, tiled=T...  3.71 us
  transfers between devices with their start and end apart: 1, of which 1 were waited for; matrix products, arithmetic and copies ran while one was open for 2% of the time, Pallas kernels for 3%

profile of v11, /device:TPU:1, one launch (start us, length us, event | category | flops | bytes accessed | tf_op | source)
XLA Modules:
  0.0 144.4 jit_solution(12626541594636639473)
XLA Ops:
  0.6 1.9 %shard_map.94 = bf16[32,4,1152]{2,1,0:T(4,128)(2,1)} custom-call(bf16[128,1024]{1,0:T(8,128)(2,1)} %bitcast.11, s32[1,128]{1,0:T(1,128)} %order_ref.3, f32[1,128]{1,0:T(1,128)} %cot_ref.1), custom_call_target="tpu_custom_call" | custom-call | tf_op jit(solution)/shard_map/pallas_call | solution.py:285
  2.5 15.9 %all-to-all-start = ((bf16[32,4,1152]{2,1,0:T(4,128)(2,1)}), bf16[32,4,1152]{2,1,0:T(4,128)(2,1)S(1)}, u32[]{:S(2)}, u32[]{:S(2)}) async-start(bf16[32,4,1152]{2,1,0:T(4,128)(2,1)} %shard_map.94), calls=%async_computation | async-start | bytes 589824 | tf_op jit(solution)/shard_map/all_to_all | solution.py:288
  18.5 0.7 broadcast_in_dim.11.bias_ref
  19.2 2.2 %shard_map.95 = bf16[128,1536]{1,0:T(8,128)(2,1)} custom-call(bf16[256,1536]{1,0:T(8,128)(2,1)} %bitcast.10, s32[1,256]{1,0:T(1,128)} %slot_ref.1), custom_call_target="tpu_custom_call" | custom-call | tf_op jit(solution)/shard_map/pallas_call | solution.py:289
  21.3 6.0 %all_gather.10.pooled_ref = bf16[256,1536]{1,0:T(8,128)(2,1)} all-gather(bf16[128,1536]{1,0:T(8,128)(2,1)} %shard_map.95), channel_id=1, replica_groups=mesh['y'=4,'h'=4,'x'=4,'l'=8,'c'=2] {'c'}, dimensions={0}, use_global_device_ids=true | all-gather | bytes 1179648 | tf_op jit(solution)/shard_map/all_gather | solution.py:292
  27.3 2.4 %shard_map.96.target_ref = bf16[256,1536]{1,0:T(8,128)(2,1)} custom-call(bf16[256,1536]{1,0:T(8,128)(2,1)} %all_gather.10.pooled_ref), custom_call_target="tpu_custom_call" | custom-call | tf_op jit(solution)/shard_map/pallas_call | solution.py:293
  29.7 2.0 %slice.3.weight_ref = bf16[1024,1408]{1,0:T(8,128)(2,1)S(1)} slice(bf16[1024,1536]{1,0:T(8,128)(2,1)} %rest_ref.1), slice={[0:1024], [0:1408]} | slice | bytes 5767168 | tf_op jit(solution)/shard_map/slice | solution.py:315
  31.8 6.7 %all-to-all-done = bf16[32,4,1152]{2,1,0:T(4,128)(2,1)S(1)} async-done(((bf16[32,4,1152]{2,1,0:T(4,128)(2,1)}), bf16[32,4,1152]{2,1,0:T(4,128)(2,1)S(1)}, u32[]{:S(2)}, u32[]{:S(2)}) %all-to-all-start) | async-done | bytes 294944 | tf_op jit(solution)/shard_map/all_to_all | solution.py:288
  38.5 0.1 reshape.15
  38.5 3.7 %all_gather.9.both_ref = bf16[256,1152]{1,0:T(8,128)(2,1)S(1)} all-gather(bf16[128,1152]{1,0:T(8,128)(2,1)S(1)} %reshape.15), channel_id=1, replica_groups=mesh['y'=4,'h'=4,'x'=4,'l'=8,'c'=2] {'c'}, dimensions={0}, use_global_device_ids=true | all-gather | bytes 884736 | tf_op jit(solution)/shard_map/all_gather | solution.py:298
  42.2 3.0 %shard_map.97 = (bf16[16,400,128]{2,1,0:T(8,128)(2,1)S(1)}, f32[40,128]{1,0:T(8,128)S(1)}) custom-call(s32[1]{0:T(128)} %bitcast.core_ref, s32[1]{0:T(128)} %bitcast.1.high_ref, bf16[256,1152]{1,0:T(8,128)(2,1)S(1)} %all_gather.9.both_ref, bf16[256,1536]{1,0:T(8,128)(2,1)} %shard_map.96.target_ref, bf16[1024,1408]{1,0:T(8,128)(2,1)S(1)} %slice.3.weight_ref, ...), custom_call_target="tpu_custom_call" | custom-call | tf_op jit(solution)/shard_map/pallas_call | solution.py:301
  45.3 0.0 copy-start
  45.3 27.0 %all_to_all.20.part_ref = bf16[16,400,128]{2,1,0:T(8,128)(2,1)S(1)} all-to-all(bf16[16,400,128]{2,1,0:T(8,128)(2,1)S(1)} %get-tuple-element.10), channel_id=1, replica_groups=mesh['y'=4,'h'=4,'x'=4,'l'=8,'c'=2] {'y','x'}, dimensions={0} | all-to-all | bytes 3276800 | tf_op jit(solution)/shard_map/all_to_all | solution.py:317
  72.3 0.3 shard_map.98
  72.6 48.5 %all_to_all.21.part_ref = bf16[32,16,128]{2,1,0:T(8,128)(2,1)S(1)} all-to-all(bf16[32,16,128]{2,1,0:T(8,128)(2,1)S(1)} %bitcast.9), channel_id=1, replica_groups=mesh['y'=4,'h'=4,'x'=4,'l'=8,'c'=2] {'h','l'}, dimensions={0} | all-to-all | bytes 262144 | tf_op jit(solution)/shard_map/all_to_all | solution.py:326
  121.0 0.1 shard_map.99
  121.1 16.6 %all_to_all.22 = bf16[32,16,128]{2,1,0:T(8,128)(2,1)S(1)} all-to-all(bf16[32,16,128]{2,1,0:T(8,128)(2,1)S(1)} %shard_map.99), channel_id=1, replica_groups=mesh['y'=4,'h'=4,'x'=4,'l'=8,'c'=2] {'x','l'}, dimensions={0} | all-to-all | bytes 262144 | tf_op jit(solution)/shard_map/all_to_all | solution.py:328
  137.7 5.7 %all_gather.11.both_ref = bf16[1024,128]{1,0:T(8,128)(2,1)S(1)} all-gather(bf16[512,128]{1,0:T(8,128)(2,1)S(1)} %bitcast.7), channel_id=1, replica_groups=mesh['y'=4,'h'=4,'x'=4,'l'=8,'c'=2] {'c'}, dimensions={0}, use_global_device_ids=true | all-gather | bytes 393216 | tf_op jit(solution)/shard_map/all_gather | solution.py:329
  143.4 0.0 copy-done
  143.4 1.0 shard_map.100
Async XLA Ops:
  2.5 35.9 %all-to-all-start = ((bf16[32,4,1152]{2,1,0:T(4,128)(2,1)}), bf16[32,4,1152]{2,1,0:T(4,128)(2,1)S(1)}, u32[]{:S(2)}, u32[]{:S(2)}) async-start(bf16[32,4,1152]{2,1,0:T(4,128)(2,1)} %shard_map.94), calls=%async_computation | async-start | bytes 589824 | tf_op jit(solution)/shard_map/all_to_all | solution.py:288
  45.3 98.1 %copy-start = (s32[1,128]{1,0:T(1,128)S(1)}, s32[1,128]{1,0:T(1,128)}, u32[]{:S(2)}) copy-start(s32[1,128]{1,0:T(1,128)} %order_ref.3) | copy-start | bytes 1540
